TPU v7x, 256 devices: a whole 4x4x8 slice. The times are simulated.
256 devices in a mesh: seq: 32 (over y, z), head: 8 (over x, core).
Axes of the slice: x: 4, y: 4, z: 8, core: 2. Of those that a mesh axis runs over, the one named last changes fastest.
Arguments:
- queries: bfloat16 [65536, 2048], P('seq', 'head'), may hold values from -2.5 to 2.5
- keys: bfloat16 [65536, 2048], P('seq', 'head'), may hold values from -2.5 to 2.5
- values: bfloat16 [65536, 2048], P('seq', 'head'), may hold values from -2.5 to 2.5
- w_out: bfloat16 [2048, 2048], P('head'), may hold values from -0.125 to 0.125
- grad_out: bfloat16 [65536, 2048], P(('seq', 'head')), may hold values from -6 to 6
Outputs:
- mixed: bfloat16 [65536, 2048], P(('seq', 'head'))
- grad_queries: bfloat16 [65536, 2048], P('seq', 'head')
- grad_keys: bfloat16 [65536, 2048], P('seq', 'head')
- grad_values: bfloat16 [65536, 2048], P('seq', 'head')
- grad_weight: bfloat16 [2048, 2048], P('head')
All inputs are finite; a program needn't handle non-finite values.
Results may differ from a plain program's by a relative error of at most 0.013.
Values may be sent and summed in bfloat16 or wider, within the bound.
No kernel may reach another device: no remote copies, remote signals or barrier semaphores. Data moves between devices by JAX's collectives and lax.ppermute only.
A program may use at most 192 MiB of HBM per device.

v0:
```python
import functools
import jax
import jax.numpy as jnp
from jax import lax
from jax.experimental import pallas as pl
from jax.experimental.pallas import tpu as pltpu
from jax.sharding import PartitionSpec as P

HD = 128
B = 128
LOCAL = 4
F32 = jnp.float32
BF16 = jnp.bfloat16
EXP_SCALE = 1.4426950408889634 * HD ** (-0.5)
SCALE = HD ** (-0.5)
VMEM = 56 * 1024 * 1024
COST = 0.05e6


def nn(a, b):
    return lax.dot_general(a, b, (((1,), (0,)), ((), ())), preferred_element_type=F32)


def nt(a, b):
    return lax.dot_general(a, b, (((1,), (1,)), ((), ())), preferred_element_type=F32)


def tn(a, b):
    return lax.dot_general(a, b, (((0,), (0,)), ((), ())), preferred_element_type=F32)


def call(kernel, micros, **kwargs):
    cost = pl.CostEstimate(flops=0, bytes_accessed=int(micros * COST), transcendentals=0)
    return pl.pallas_call(
        kernel,
        cost_estimate=cost,
        compiler_params=pltpu.CompilerParams(vmem_limit_bytes=VMEM),
        **kwargs,
    )


def offset(level, tokens):
    return tokens - (tokens >> (level - 1))


def spec(rows, block=0):
    return pl.BlockSpec((rows, HD), lambda h: (block, h))


def lead(rows, width):
    return pl.BlockSpec((1, rows, width), lambda h: (h, 0, 0))


def both(rows):
    return pl.BlockSpec((rows, 2 * HD), lambda h: (0, h))


def with_ones(v):
    return jnp.concatenate([v, jnp.ones(v.shape, BF16)], axis=1)


def repeat2(x, scratch, base=0):
    n = x.shape[0]
    scratch[pl.ds(base, n, stride=2), :] = x
    scratch[pl.ds(base + 1, n, stride=2), :] = x


def coarsen_kernel(q_ref, k_ref, v_ref, qc_ref, kc_ref, vc_ref, m1_ref, m2_ref):
    tokens = q_ref.shape[0]
    r = lax.broadcasted_iota(jnp.int32, (B, 2 * B), 0)
    c = lax.broadcasted_iota(jnp.int32, (B, 2 * B), 1)
    mean = jnp.where(c // 2 == r, 0.5, 0.0).astype(BF16)
    half = mean[:64, :128]
    for src, dst in ((q_ref, qc_ref), (k_ref, kc_ref), (v_ref, vc_ref)):
        for i in range(tokens // 256):
            dst[i * B:(i + 1) * B, :] = nn(mean, src[i * 256:(i + 1) * 256, :]).astype(BF16)
    for level in range(2, LOCAL + 1):
        before, here = offset(level - 1, tokens), offset(level, tokens)
        for dst in (qc_ref, kc_ref, vc_ref):
            for i in range((tokens >> level) // B):
                rows = dst[before + i * 256:before + (i + 1) * 256, :]
                dst[here + i * B:here + (i + 1) * B, :] = nn(mean, rows).astype(BF16)
    tail = offset(LOCAL + 1, tokens)
    for dst in (qc_ref, kc_ref, vc_ref):
        x5 = nn(half, dst[tail - B:tail, :]).astype(BF16)
        x6 = nn(half[:32, :64], x5).astype(BF16)
        x7 = nn(half[:16, :32], x6).astype(BF16)
        x8 = nn(half[:16, :16], x7).astype(BF16)
        dst[tail:tail + 64, :] = x5
        dst[tail + 64:tail + 96, :] = x6
        dst[tail + 96:tail + 112, :] = x7
        dst[tail + 112:tail + 128, :] = x8
    tail = tokens - 64
    for lane, src in ((0, kc_ref), (HD, vc_ref)):
        columns = slice(lane, lane + HD)
        m1_ref[:B, columns] = src[tokens - 256:tokens - 128, :]
        m2_ref[:64, columns] = src[tokens - 128:tail, :]
        m1_ref[B:, columns] = src[tail:, :]
        m2_ref[64:, columns] = src[tail:, :]


def coarsen(q, k, v):
    shape = jax.ShapeDtypeStruct(q.shape, BF16)
    tokens, width = q.shape
    sizes = (192, 128)
    return call(
        coarsen_kernel,
        6,
        grid=(width // HD,),
        in_specs=[spec(tokens)] * 3,
        out_specs=[spec(tokens)] * 3 + [both(n) for n in sizes],
        out_shape=[shape] * 3 + [jax.ShapeDtypeStruct((n, 2 * width), BF16) for n in sizes],
        name="coarsen",
    )(q, k, v)


def forward_blocks(blocks):
    scores = [nt(q, k) for q, k, _ in blocks]
    expos = [jnp.exp2(x * EXP_SCALE).astype(BF16) for x in scores]
    return [nn(e, with_ones(v)) for e, (_, _, v) in zip(expos, blocks)]


def sibling_pairs(level, tokens):
    off = offset(level, tokens)
    for i in range(0, tokens >> level, 256):
        lo, hi = (off + i, i), (off + i + B, i + B)
        yield lo, hi
        yield hi, lo


def local_forward_kernel(q_ref, k_ref, v_ref, qc_ref, kc_ref, vc_ref, numer_ref, total_ref, *scr):
    tokens = q_ref.shape[0]
    for levels in ((3, 2), (1,)):
        pairs = [(level, *pair) for level in levels for pair in sibling_pairs(level, tokens)]
        blocks = []
        for _, (ma, _), (oa, _) in pairs:
            mine, other = slice(ma, ma + B), slice(oa, oa + B)
            blocks.append((qc_ref[mine, :], kc_ref[other, :], vc_ref[other, :]))
        for (level, (_, at), _), u in zip(pairs, forward_blocks(blocks)):
            n, t = u[:, :HD], u[:, HD:]
            if level < LOCAL - 1:
                n = n + 2.0 * scr[2 * level][at:at + B, :]
                t = t + 2.0 * scr[2 * level + 1][at:at + B, :]
            repeat2(n, scr[2 * level - 2], 2 * at)
            repeat2(t, scr[2 * level - 1], 2 * at)
    for i in range(0, tokens, 1024):
        rows = [slice(at, at + 256) for at in range(i, i + 1024, 256)]
        sums = forward_blocks([(q_ref[r, :], k_ref[r, :], v_ref[r, :]) for r in rows])
        for r, u in zip(rows, sums):
            numer_ref[0, r, :] = u[:, :HD] + 2.0 * scr[0][r, :]
            total_ref[0, r, :] = u[:, HD:] + 2.0 * scr[1][r, :]


def local_forward(head, q, k, v, qc, kc, vc):
    tokens, width = q.shape
    scratch = []
    for level in range(1, LOCAL):
        scratch += [pltpu.VMEM((tokens >> (level - 1), HD), F32)] * 2
    columns = pl.BlockSpec((tokens, HD), lambda i: (0, head))
    return call(
        local_forward_kernel,
        5,
        grid=(1,),
        in_specs=[columns] * 6,
        out_specs=[lead(tokens, HD)] * 2,
        out_shape=[jax.ShapeDtypeStruct((1, tokens, HD), F32)] * 2,
        scratch_shapes=scratch,
        name="local_forward",
    )(q, k, v, qc, kc, vc)


def level_of_row(row):
    steps = [(row >= edge).astype(jnp.int32) for edge in (128, 192, 224, 240, 248)]
    return sum(steps)


KEYS = 640
ARRIVED = (192, 128, 128, 160, 96, 96, 128)
USED = (128, 64, 64, 128, 64, 64, 128)


def spread_levels(packed, scratch, weight):
    bounds = (0, 128, 192, 224, 240, 248)
    x = packed[240:248, :]
    for i in range(3, -1, -1):
        lo, hi = bounds[i], bounds[i + 1]
        repeat2(x, scratch)
        x = packed[lo:hi, :] + weight * scratch[0:hi - lo, :]
    return x


def repeat16(x):
    high = x.astype(BF16)
    low = (x - high.astype(F32)).astype(BF16)
    r = lax.broadcasted_iota(jnp.int32, (256, 32), 0)
    c = lax.broadcasted_iota(jnp.int32, (256, 32), 1)
    copies = jnp.where((r >> 4) == (c & 15), 1.0, 0.0).astype(BF16)
    for i in range(x.shape[0] // 16):
        part = slice(i * 16, i * 16 + 16)
        yield slice(i * 256, i * 256 + 256), nn(copies, jnp.concatenate([high[part], low[part]], axis=0))


def coarse_forward_kernel(numer0, total0, numer1, total1, q_ref, *refs):
    arrived, (att_ref, rtot_ref, side_ref, small) = refs[:7], refs[7:]
    at = 0
    for ref, n in zip(arrived, USED):
        side_ref[at:at + n, :] = ref[:n, :]
        at += n
    rows = q_ref.shape[0]
    level = level_of_row(lax.broadcasted_iota(jnp.int32, (rows, KEYS), 0))
    other = lax.broadcasted_iota(jnp.int32, (rows, KEYS), 1) // B
    expos = jnp.where(level == other, jnp.exp2(nt(q_ref[...], side_ref[:, :HD]) * EXP_SCALE), 0.0)
    u = nn(expos.astype(BF16), with_ones(side_ref[:, HD:]))
    parts = [16.0 * spread_levels(u[:, half], small, 2.0) for half in (slice(0, HD), slice(HD, None))]
    coarse = jnp.concatenate(parts, axis=1)
    for head, numer_ref, total_ref in ((0, numer0, total0), (1, numer1, total1)):

        @pl.when(pl.program_id(0) == head)
        def _():
            for at, x in repeat16(coarse):
                rtot = 1.0 / (total_ref[0, at, :] + x[:, HD:])
                rtot_ref[0, at, :] = rtot
                att_ref[at, :] = ((numer_ref[0, at, :] + x[:, :HD]) * rtot).astype(BF16)


def coarse_forward(local, qc, arrived):
    tokens, width = qc.shape
    heads = width // HD
    whole = pl.BlockSpec((1, tokens, HD), lambda h: (0, 0, 0))
    return call(
        coarse_forward_kernel,
        6,
        grid=(heads,),
        in_specs=[whole] * 4
        + [spec(256, tokens // 256 - 1)]
        + [both(n) for n in ARRIVED],
        out_specs=[spec(tokens), lead(tokens, HD), both(KEYS)],
        out_shape=[
            jax.ShapeDtypeStruct((tokens, heads * HD), BF16),
            jax.ShapeDtypeStruct((heads, tokens, HD), F32),
            jax.ShapeDtypeStruct((KEYS, 2 * heads * HD), BF16),
        ],
        scratch_shapes=[pltpu.VMEM((B, HD), F32)],
        name="coarse_forward",
    )(*local, qc, *arrived)


def with_dot(g, dot):
    lane = lax.broadcasted_iota(jnp.int32, dot.shape, 1)
    high = (-dot).astype(BF16)
    low = (-dot - high.astype(F32)).astype(BF16)
    zero = jnp.zeros(dot.shape, BF16)
    parts = jnp.where(lane == 0, high, jnp.where(lane == 1, low, zero))
    return jnp.concatenate([g.astype(BF16), parts], axis=1)


def backward_blocks(blocks, mask=None):
    scores = [nt(k, q) for q, k, _, _ in blocks]
    probes = [nt(with_ones(v), g) for _, _, v, g in blocks]
    expos = [jnp.exp2(x * EXP_SCALE) for x in scores]
    if mask is not None:
        expos = [jnp.where(mask, e, 0.0) for e in expos]
    slopes = [(e * p).astype(BF16) for e, p in zip(expos, probes)]
    dv = [nn(e.astype(BF16), g[:, :HD]) for e, (_, _, _, g) in zip(expos, blocks)]
    dk = [nn(s, q) for s, (q, _, _, _) in zip(slopes, blocks)]
    dq = [tn(s, k) for s, (_, k, _, _) in zip(slopes, blocks)]
    return list(zip(dq, dk, dv))


def coarse_backward_kernel(
    ga_ref, att_ref, rtot_ref, q_ref, side_ref, g0_ref, gc_ref, dq_ref, *refs
):
    sent, (g_scr, d_scr, small) = refs[:5], refs[5:]
    tokens = ga_ref.shape[0]
    step = 256
    for i in range(tokens // step):
        rows = slice(i * step, (i + 1) * step)
        ga = ga_ref[rows, :].astype(F32)
        rtot = rtot_ref[0, rows, :]
        g = ga * rtot
        dot = jnp.sum(ga * att_ref[rows, :].astype(F32), axis=1, keepdims=True) * rtot
        g_scr[rows, :] = g
        d_scr[rows, :] = dot
        g0_ref[0, rows, :] = with_dot(g, dot)
    for level in range(1, 9):
        n = tokens >> level
        here = offset(level, tokens)
        chunk = min(n, 256)
        for i in range(n // chunk):
            even, odd = pl.ds(2 * i * chunk, chunk, stride=2), pl.ds(2 * i * chunk + 1, chunk, stride=2)
            g = g_scr[even, :] + g_scr[odd, :]
            dot = d_scr[even, :] + d_scr[odd, :]
            g_scr[i * chunk:(i + 1) * chunk, :] = g
            d_scr[i * chunk:(i + 1) * chunk, :] = dot
            if n < 16:
                pad = jnp.zeros((16 - n, HD), F32)
                g, dot = jnp.concatenate([g, pad], axis=0), jnp.concatenate([dot, pad], axis=0)
            gc_ref[0, here + i * chunk:here + i * chunk + g.shape[0], :] = with_dot(g, dot)
    rows = q_ref.shape[0]
    level = level_of_row(lax.broadcasted_iota(jnp.int32, (KEYS, rows), 1))
    other = lax.broadcasted_iota(jnp.int32, (KEYS, rows), 0) // B
    g = gc_ref[0, tokens - rows:tokens, :]
    block = (q_ref[...], side_ref[:, :HD], side_ref[:, HD:], g)
    (dq, dk, dv), = backward_blocks([block], level == other)
    dq_ref[0] = spread_levels(dq, small, 1.0)
    for lane, d in ((0, (dk * SCALE).astype(BF16)), (HD, dv.astype(BF16))):
        for i, ref in enumerate(sent):
            ref[:, lane:lane + HD] = d[i * B:(i + 1) * B, :]


def coarse_backward(ga, att, rtot, qc, side):
    heads, tokens, _ = rtot.shape
    wide = jax.ShapeDtypeStruct((heads, tokens, 2 * HD), BF16)
    return call(
        coarse_backward_kernel,
        6,
        grid=(heads,),
        in_specs=[spec(tokens)] * 2 + [lead(tokens, HD), spec(256, tokens // 256 - 1), both(KEYS)],
        out_specs=[lead(tokens, 2 * HD)] * 2 + [lead(B, HD)] + [both(B)] * 5,
        out_shape=[wide, wide, jax.ShapeDtypeStruct((heads, B, HD), F32)]
        + [jax.ShapeDtypeStruct((B, 2 * heads * HD), BF16)] * 5,
        scratch_shapes=[pltpu.VMEM((tokens, HD), F32)] * 2 + [pltpu.VMEM((B, HD), F32)],
        name="coarse_backward",
    )(ga, att, rtot, qc, side)


SCRATCH = 3 * (LOCAL - 1) + 1


def local_backward_kernel(
    q_ref, k_ref, v_ref, qc_ref, kc_ref, vc_ref, g0_ref, gc_ref, dq4_ref, *refs
):
    (dq_ref, dk_ref, dv_ref), scr = refs[-SCRATCH - 3:-SCRATCH], refs[-SCRATCH:]
    tokens = q_ref.shape[0]
    repeat2(dq4_ref[0], scr[3 * (LOCAL - 1)])
    for levels in ((3, 2), (1,)):
        pairs = [(level, *pair) for level in levels for pair in sibling_pairs(level, tokens)]
        blocks = []
        for _, (ma, _), (oa, _) in pairs:
            mine, other = slice(ma, ma + B), slice(oa, oa + B)
            blocks.append((qc_ref[mine, :], kc_ref[other, :], vc_ref[other, :], gc_ref[0, mine, :]))
        for (level, (_, mr), (_, orow)), (dq, dk, dv) in zip(pairs, backward_blocks(blocks)):
            dq = dq + scr[3 * level][mr:mr + B, :]
            if level < LOCAL - 1:
                dk = dk + scr[3 * level + 1][orow:orow + B, :]
                dv = dv + scr[3 * level + 2][orow:orow + B, :]
            repeat2(dq, scr[3 * level - 3], 2 * mr)
            repeat2(dk, scr[3 * level - 2], 2 * orow)
            repeat2(dv, scr[3 * level - 1], 2 * orow)
    for i in range(0, tokens, 512):
        rows = [slice(at, at + 256) for at in range(i, i + 512, 256)]
        blocks = [(q_ref[r, :], k_ref[r, :], v_ref[r, :], g0_ref[0, r, :]) for r in rows]
        for r, (dq, dk, dv) in zip(rows, backward_blocks(blocks)):
            dq_ref[r, :] = ((dq + scr[0][r, :]) * SCALE).astype(BF16)
            dk_ref[r, :] = ((dk + scr[1][r, :]) * SCALE).astype(BF16)
            dv_ref[r, :] = (dv + scr[2][r, :]).astype(BF16)


def local_backward(head, inputs, before=()):
    tokens, width = inputs[0].shape
    scratch = []
    for level in range(1, LOCAL):
        scratch += [pltpu.VMEM((tokens >> (level - 1), HD), F32)] * 3
    scratch += [pltpu.VMEM((tokens >> (LOCAL - 1), HD), F32)]
    columns = pl.BlockSpec((tokens, HD), lambda i: (0, head))
    wide = pl.BlockSpec((1, tokens, 2 * HD), lambda i: (head, 0, 0))
    small = pl.BlockSpec((1, B, HD), lambda i: (head, 0, 0))
    return call(
        local_backward_kernel,
        8,
        grid=(1,),
        in_specs=[columns] * 6 + [wide] * 2 + [small] + [pl.BlockSpec(memory_space=pl.ANY)] * len(before),
        out_specs=[columns] * 3,
        out_shape=[jax.ShapeDtypeStruct((tokens, width), BF16)] * 3,
        scratch_shapes=scratch,
        input_output_aliases={9 + i: i for i in range(len(before))},
        name="local_backward",
    )(*inputs, *before)


def finish_kernel(dk_ref, dv_ref, own, r1, r2, r3, gk_ref, gv_ref, small):
    rows = lambda ref, lo, hi: ref[lo:hi, :].astype(F32)
    x4 = rows(r1, 0, 128)
    x5 = rows(r2, 0, 64) + rows(r3, 0, 64)
    rest = rows(own, 0, 64) + rows(r1, 128, 192) + rows(r2, 64, 128) + rows(r3, 64, 128)
    packed = jnp.concatenate([x4, x5, rest], axis=0)
    parts = [spread_levels(packed[:, half], small, 1.0) for half in (slice(0, HD), slice(HD, None))]
    for at, x in repeat16(jnp.concatenate(parts, axis=1)):
        gk_ref[at, :] = (dk_ref[at, :].astype(F32) + x[:, :HD]).astype(BF16)
        gv_ref[at, :] = (dv_ref[at, :].astype(F32) + x[:, HD:]).astype(BF16)


def finish(dk, dv, returned):
    tokens, width = dk.shape
    shape = jax.ShapeDtypeStruct((tokens, width), BF16)
    return call(
        finish_kernel,
        4,
        grid=(width // HD,),
        in_specs=[spec(tokens)] * 2 + [both(n) for n in (64, 256, 128, 128)],
        out_specs=[spec(tokens)] * 2,
        out_shape=[shape] * 2,
        scratch_shapes=[pltpu.VMEM((B, HD), F32)],
        name="finish",
    )(dk, dv, *returned)


def mix_kernel(att_ref, w_ref, out_ref, held, sem):
    shards, _, width = att_ref.shape
    chunk = 512
    copies = []
    for c in range(out_ref.shape[1] // chunk):
        columns = pl.ds(c * chunk, chunk)
        copies.append(pltpu.make_async_copy(w_ref.at[:, columns], held.at[:, columns], sem.at[c]))
        copies[-1].start()
    att = jnp.concatenate([att_ref[j] for j in range(shards)], axis=1)
    for c, copy in enumerate(copies):
        columns = slice(c * chunk, (c + 1) * chunk)
        copy.wait()
        out_ref[:, columns] = nn(att, held[:, columns]).astype(BF16)


def mix(att, w):
    shards, rows, width = att.shape
    whole = pl.BlockSpec(memory_space=pltpu.VMEM)
    return call(
        mix_kernel,
        6,
        in_specs=[whole, pl.BlockSpec(memory_space=pl.ANY)],
        out_specs=whole,
        out_shape=jax.ShapeDtypeStruct((rows, w.shape[1]), BF16),
        scratch_shapes=[pltpu.VMEM(w.shape, BF16), pltpu.SemaphoreType.DMA((w.shape[1] // 512,))],
        name="mix",
    )(att, w)


def swap(x, axis, distance):
    return lax.ppermute(x, axis, [(i, i ^ distance) for i in range(lax.axis_size(axis))])


def swap_z(x, distance):
    place = lambda i: (i & 24) | ((((i - 2) & 7) ^ distance) + 2) & 7
    return lax.ppermute(x, "seq", [(i, place(i)) for i in range(lax.axis_size("seq"))])


def shift_y(x, distance):
    n = lax.axis_size("seq")
    return lax.ppermute(x, "seq", [(i, (i + 8 * distance) % n) for i in range(n)])


def after(x, *others):
    return lax.optimization_barrier((x,) + others)[0]


def cat(parts):
    return jnp.concatenate(parts, axis=0)


def levels_of(x):
    n = x.shape[0]
    return x[n - 64:n - 32], x[n - 32:n - 16], x[n - 16:n - 8]


def add(*parts):
    return sum(x.astype(F32) for x in parts).astype(BF16)


def quarters(x, place, axis):
    n = x.shape[axis] // 4
    return [lax.dynamic_slice_in_dim(x, (place ^ j) * n, n, axis) for j in range(4)]


def join_quarters(parts, places, axis):
    n = parts[0].shape[axis]
    whole = jnp.concatenate([jnp.zeros(p.shape, p.dtype) for p in parts], axis)
    for place, part in zip(places, parts):
        whole = lax.dynamic_update_slice_in_dim(whole, part, place * n, axis)
    return whole


def body(queries, keys, values, w_out, grad_out):
    tokens, width = queries.shape
    shards = lax.axis_size("head")
    assert shards == 8 and lax.axis_size("seq") == 32
    y, z = lax.axis_index("seq") >> 3, (lax.axis_index("seq") - 2) & 7
    z = (z & 3) ^ (3 * (z >> 2))
    cotangent = lax.all_gather(grad_out, "head", axis=0, tiled=True)
    w_full = lax.all_gather(w_out, "head", axis=0, tiled=True)

    qc, kc, vc, m1, m2 = coarsen(queries, keys, values)
    near = [swap(m1, "seq", 1), swap(m2, "seq", 2), swap(m2, "seq", 3)]
    inputs = (queries, keys, values, qc, kc)
    local = tuple(local_forward(0, *inputs, vc))
    near = after(tuple(near), local[0])
    six, seven, eight = (cat(parts) for parts in zip(*[levels_of(x) for x in (m1, *near)]))
    group = cat([seven, eight])
    far = [swap(cat([six, eight]), "seq", 7), swap(group, "seq", 8), swap(group, "seq", 15)]
    local += tuple(local_forward(1, *inputs, after(vc, six)))
    far = after(tuple(far), local[2])
    last = swap(cat([eight] + [x[x.shape[0] - 32:] for x in far]), "seq", 24)
    attended, rtot, side = coarse_forward(local, qc, (*near, *far, last))

    mine = lax.all_to_all(attended.reshape(shards, tokens // shards, width), "head", 0, 0)
    grad_weight = tn(attended, cotangent).astype(BF16)
    ga = nt(cotangent, after(w_out, grad_weight)).astype(BF16)
    own, *rest = quarters(grad_weight, y, 1)
    rest = [swap(x, "seq", 8 * (j + 1)) for j, x in enumerate(rest)]
    g0, gc, dq4, e4, e5, e6, e7, e8 = coarse_backward(ga, attended, rtot, qc, side)
    rest = after(tuple(rest), dq4)
    partial = add(own, *rest)
    mine = after(mine, dq4)

    x8 = swap(e8, "seq", 24)
    own, *rest = quarters(partial, z, 0)
    rest = [swap_z(x, j + 1) for j, x in enumerate(rest)]
    inputs = (queries, keys, values, qc, kc, vc, g0, gc)
    done = local_backward(0, inputs + (after(dq4, partial),))
    rest, x8 = after((rest, x8), done[0])
    partial = add(own, *rest)

    f7 = swap(cat([e6, x8[32:64]]), "seq", 7)
    f8 = swap(cat([e7[:64], x8[64:96]]), "seq", 8)
    f15 = swap(cat([e7[64:], x8[96:]]), "seq", 15)
    low = swap_z(partial, 7)
    grad_q, dk, dv = local_backward(1, inputs + (after(dq4, partial, x8),), done)
    low, f7, f8, f15 = after((low, f7, f8, f15), grad_q)
    partial = add(partial, low)

    x6, x7, x8 = f7[:B], add(f8[:64], f15[:64]), add(x8[:32], f7[B:], f8[64:], f15[64:])
    first = [e4, e5[:64], e5[64:]]
    pad = jnp.zeros((8, x8.shape[1]), BF16)
    tails = [cat([x6[32 * j:][:32], x7[16 * j:][:16], x8[8 * j:][:8], pad]) for j in range(4)]
    messages = [[x, tails[j + 1]] for j, x in enumerate(first)]
    messages[0].append(partial)
    near = [swap(cat(x), "seq", j + 1) for j, x in enumerate(messages)]
    rest = [swap_z(partial, j) for j in (2, 3)]
    mixed = mix(after(mine, partial, tails[0]), w_full)
    near, rest = after((near, rest), mixed)
    summed = join_quarters([partial, near[0][192:]] + rest, [z ^ j for j in range(4)], 0)

    up, down = shift_y(summed, 1), shift_y(summed, -1)
    grad_k, grad_v = finish(after(dk, summed), dv, (tails[0], *near))
    up, down = after((up, down), grad_k)
    far = cat([shift_y(up[:B], 1), shift_y(down[B:], -1)])
    places = [y, (y + 3) & 3, (y + 1) & 3, (y + 2) & 3]
    return mixed, grad_q, grad_k, grad_v, join_quarters([summed, up, down, far], places, 1)


def solution(mesh):
    return jax.shard_map(
        body,
        mesh=mesh,
        in_specs=(
            P("seq", "head"),
            P("seq", "head"),
            P("seq", "head"),
            P("head", None),
            P(("seq", "head"), None),
        ),
        out_specs=(
            P(("seq", "head"), None),
            P("seq", "head"),
            P("seq", "head"),
            P("seq", "head"),
            P("head", None),
        ),
        check_vma=False,
    )
```

profile of v0, /device:TPU:16, one launch (start us, length us, event | category | flops | bytes accessed | tf_op | source)
XLA Modules:
  0.0 162.3 jit_solution(2123035906550578136)
XLA Ops:
  7.2 0.7 all-gather.3.cloned.1.call-update
  7.9 0.7 all-gather.5.cloned.1.call-update
  8.6 6.4 %coarsen.1 = (bf16[2048,256]{1,0:T(8,128)(2,1)}, bf16[2048,256]{1,0:T(8,128)(2,1)}, bf16[2048,256]{1,0:T(8,128)(2,1)}, bf16[192,512]{1,0:T(8,128)(2,1)}, bf16[128,512]{1,0:T(8,128)(2,1)}) custom-call(bf16[2048,256]{1,0:T(8,128)(2,1)} %q_ref.9, bf16[2048,256]{1,0:T(8,128)(2,1)} %k_ref.9, bf16[2048,256]{1,0:T(8,128)(2,1)} %v_ref.9), custom_call_target="tpu_custom_call" | custom-call | bytes 300000 | tf_op jit(solution)/shard_map/coarsen/pallas_call | solution.py:106
  15.1 3.3 %collective-permute-start.1 = (bf16[128,512]{1,0:T(8,128)(2,1)}, bf16[128,512]{1,0:T(8,128)(2,1)S(1)}, u32[]{:S(2)}, u32[]{:S(2)}) collective-permute-start(bf16[128,512]{1,0:T(8,128)(2,1)} %get-tuple-element.71), channel_id=1, source_target_pairs={{0,16},{8,24},{16,0},{24,8},{32,48},{40,56},{48,32},{56,40},{64,80... | collective-permute-start | bytes 393224 | tf_op jit(solution)/shard_map/ppermute | solution.py:438
  18.3 1.4 collective-permute-start.2
  20.3 4.4 %local_forward.2 = (f32[1,2048,128]{2,1,0:T(8,128)}, f32[1,2048,128]{2,1,0:T(8,128)}) custom-call(bf16[2048,256]{1,0:T(8,128)(2,1)} %q_ref.9, bf16[2048,256]{1,0:T(8,128)(2,1)} %k_ref.9, bf16[2048,256]{1,0:T(8,128)(2,1)} %v_ref.9, bf16[2048,256]{1,0:T(8,128)(2,1)} %get-tuple-element.63.qc_ref.q_ref, bf16[2048,256]{1,0:T(8,128)(2,1)} %get-tuple-element.64.kc_ref, ...), custom_call_target="tpu_custom_call" | custom-call | bytes 250000 | tf_op jit(solution)/shard_map/local_forward/pallas_call | solution.py:160
  24.7 0.8 constant_dynamic-update-slice_fusion.7
  25.5 0.7 constant_dynamic-update-slice_fusion.15
  26.2 2.3 %collective-permute-done.1.refs_1_ = bf16[128,512]{1,0:T(8,128)(2,1)S(1)} collective-permute-done((bf16[128,512]{1,0:T(8,128)(2,1)}, bf16[128,512]{1,0:T(8,128)(2,1)S(1)}, u32[]{:S(2)}, u32[]{:S(2)}) %collective-permute-start.1) | collective-permute-done | bytes 131104 | tf_op jit(solution)/shard_map/ppermute | solution.py:438
  28.5 2.0 %collective-permute-done.refs_0_ = bf16[192,512]{1,0:T(8,128)(2,1)S(1)} collective-permute-done((bf16[192,512]{1,0:T(8,128)(2,1)}, bf16[192,512]{1,0:T(8,128)(2,1)S(1)}, u32[]{:S(2)}, u32[]{:S(2)}) %collective-permute-start) | collective-permute-done | bytes 196640 | tf_op jit(solution)/shard_map/ppermute | solution.py:438
  30.6 0.7 constant_dynamic-update-slice_fusion.22
  31.3 5.2 %collective-permute-start.3 = (bf16[160,512]{1,0:T(8,128)(2,1)S(1)}, bf16[160,512]{1,0:T(8,128)(2,1)S(1)}, u32[]{:S(2)}, u32[]{:S(2)}) collective-permute-start(bf16[160,512]{1,0:T(8,128)(2,1)S(1)} %get-tuple-element.148), channel_id=1, source_target_pairs={{0,56},{8,48},{16,40},{24,32},{32,24},{40,16},{48,8},{56,0},{64,12... | collective-permute-start | bytes 491528 | tf_op jit(solution)/shard_map/ppermute | solution.py:438
  36.5 1.3 collective-permute-start.4
  38.1 4.6 %local_forward.3 = (f32[1,2048,128]{2,1,0:T(8,128)}, f32[1,2048,128]{2,1,0:T(8,128)}) custom-call(bf16[2048,256]{1,0:T(8,128)(2,1)} %q_ref.9, bf16[2048,256]{1,0:T(8,128)(2,1)} %k_ref.9, bf16[2048,256]{1,0:T(8,128)(2,1)} %v_ref.9, bf16[2048,256]{1,0:T(8,128)(2,1)} %get-tuple-element.63.qc_ref.q_ref, bf16[2048,256]{1,0:T(8,128)(2,1)} %get-tuple-element.64.kc_ref, ...), custom_call_target="tpu_custom_call" | custom-call | bytes 250000 | tf_op jit(solution)/shard_map/local_forward/pallas_call | solution.py:160
  42.7 5.8 %collective-permute-done.5.refs_5_ = bf16[96,512]{1,0:T(8,128)(2,1)S(1)} collective-permute-done((bf16[96,512]{1,0:T(8,128)(2,1)S(1)}, bf16[96,512]{1,0:T(8,128)(2,1)S(1)}, u32[]{:S(2)}, u32[]{:S(2)}) %collective-permute-start.5) | collective-permute-done | bytes 98336 | tf_op jit(solution)/shard_map/ppermute | solution.py:438
  48.7 4.9 %collective-permute-done.6.refs_6_ = bf16[128,512]{1,0:T(8,128)(2,1)S(1)} collective-permute-done((bf16[128,512]{1,0:T(8,128)(2,1)S(1)}, bf16[128,512]{1,0:T(8,128)(2,1)S(1)}, u32[]{:S(2)}, u32[]{:S(2)}) %collective-permute-start.6) | collective-permute-done | bytes 131104 | tf_op jit(solution)/shard_map/ppermute | solution.py:438
  54.2 6.0 %coarse_forward.1 = (bf16[2048,256]{1,0:T(8,128)(2,1)}, f32[2,2048,128]{2,1,0:T(8,128)}, bf16[640,512]{1,0:T(8,128)(2,1)}) custom-call(f32[1,2048,128]{2,1,0:T(8,128)} %get-tuple-element.66.numer0, f32[1,2048,128]{2,1,0:T(8,128)} %get-tuple-element.67.total0, f32[1,2048,128]{2,1,0:T(8,128)} %get-tuple-element.68.numer1, ...), custom_call_target="tpu_custom_call" | custom-call | bytes 300000 | tf_op jit(solution)/shard_map/coarse_forward/pallas_call | solution.py:230
  60.2 4.3 %all-to-all-start = ((bf16[8,256,256]{2,1,0:T(8,128)(2,1)}), bf16[8,256,256]{2,1,0:T(8,128)(2,1)S(1)}, u32[]{:S(2)}, u32[]{:S(2)}) async-start(bf16[8,256,256]{2,1,0:T(8,128)(2,1)} %bitcast.7), calls=%async_computation | async-start | bytes 2097152 | tf_op jit(solution)/shard_map/all_to_all | solution.py:503
  64.9 6.2 %convolution_convert_fusion.1 = bf16[256,2048]{1,0:T(8,128)(2,1)S(1)} fusion(bf16[2048,256]{1,0:T(8,128)(2,1)} %get-tuple-element.78.att_ref, bf16[2048,2048]{1,0:T(8,128)(2,1)} %all-gather.3.cloned.1.call-done), kind=kOutput, calls=%fused_computation.1 | convolution fusion | flops 2148007936 | bytes 10485760 | tf_op jit(solution)/shard_map/dot_general | solution.py:29
  71.2 1.7 %collective-permute-start.7 = (bf16[256,512]{1,0:T(8,128)(2,1)S(1)}, bf16[256,512]{1,0:T(8,128)(2,1)S(1)}, u32[]{:S(2)}, u32[]{:S(2)}) collective-permute-start(bf16[256,512]{1,0:T(8,128)(2,1)S(1)} %get-tuple-element.125), channel_id=1, source_target_pairs={{0,64},{8,72},{16,80},{24,88},{32,96},{40,104},{48,112},{56,120},{... | collective-permute-start | bytes 786440 | tf_op jit(solution)/shard_map/ppermute | solution.py:438
  73.3 1.5 collective-permute-start.9
  74.8 3.4 %fusion.ga_ref = bf16[2048,256]{1,0:T(8,128)(2,1)} fusion(bf16[256,2048]{1,0:T(8,128)(2,1)S(1)} %copy-done.2, bf16[2048,2048]{1,0:T(8,128)(2,1)S(1)} %copy-done), kind=kOutput, calls=%fused_computation.2 | convolution fusion | flops 2148007936 | bytes 10485760 | tf_op jit(solution)/shard_map/dot_general | solution.py:25
  78.2 5.9 %coarse_backward.1 = (bf16[2,2048,256]{2,1,0:T(8,128)(2,1)}, bf16[2,2048,256]{2,1,0:T(8,128)(2,1)}, f32[2,128,128]{2,1,0:T(8,128)}, bf16[128,512]{1,0:T(8,128)(2...) custom-call(bf16[2048,256]{1,0:T(8,128)(2,1)} %fusion.ga_ref, ...), custom_call_target="tpu_custom_call" | custom-call | bytes 300000 | tf_op jit(solution)/shard_map/coarse_backward/pallas_call | solution.py:314
  84.1 0.6 collective-permute-start.13
  84.7 0.9 fusion.1
  85.6 1.7 %collective-permute-done.9 = bf16[256,512]{1,0:T(8,128)(2,1)S(1)} collective-permute-done((bf16[256,512]{1,0:T(8,128)(2,1)S(1)}, bf16[256,512]{1,0:T(8,128)(2,1)S(1)}, u32[]{:S(2)}, u32[]{:S(2)}) %collective-permute-start.9) | collective-permute-done | bytes 262176 | tf_op jit(solution)/shard_map/ppermute | solution.py:438
  87.5 1.5 collective-permute-start.10
  89.0 3.6 %collective-permute-start.11 = (bf16[64,512]{1,0:T(8,128)(2,1)S(1)}, bf16[64,512]{1,0:T(8,128)(2,1)S(1)}, u32[]{:S(2)}, u32[]{:S(2)}) collective-permute-start(bf16[64,512]{1,0:T(8,128)(2,1)S(1)} %get-tuple-element.127), channel_id=1, source_target_pairs={{0,48},{8,56},{16,32},{24,40},{32,16},{40,24},{48,0},{56,8},{64,11... | collective-permute-start | bytes 196616 | tf_op jit(solution)/shard_map/ppermute | solution.py:443
  92.6 0.9 constant_dynamic-update-slice_fusion.38
  93.5 7.4 %local_backward.2 = (bf16[2048,256]{1,0:T(8,128)(2,1)}, bf16[2048,256]{1,0:T(8,128)(2,1)}, bf16[2048,256]{1,0:T(8,128)(2,1)}) custom-call(bf16[2048,256]{1,0:T(8,128)(2,1)} %q_ref.9, bf16[2048,256]{1,0:T(8,128)(2,1)} %k_ref.9, bf16[2048,256]{1,0:T(8,128)(2,1)} %v_ref.9, bf16[2048,256]{1,0:T(8,128)(2,1)} %get-tuple-element.63.qc_ref.q_ref, ...), custom_call_target="tpu_custom_call" | custom-call | bytes 400000 | tf_op jit(solution)/shard_map/local_backward/pallas_call | solution.py:368
  101.0 5.3 %collective-permute-start.17 = (bf16[96,512]{1,0:T(8,128)(2,1)S(1)}, bf16[96,512]{1,0:T(8,128)(2,1)S(1)}, u32[]{:S(2)}, u32[]{:S(2)}) collective-permute-start(bf16[96,512]{1,0:T(8,128)(2,1)S(1)} %pad_maximum_fusion.2), channel_id=1, source_target_pairs={{0,120},{8,112},{16,104},{24,96},{32,88},{40,80},{48,72},{56,64},{... | collective-permute-start | bytes 294920 | tf_op jit(solution)/shard_map/ppermute | solution.py:438
  106.4 0.7 collective-permute-start.15
  107.1 2.9 %collective-permute-start.14 = (bf16[64,512]{1,0:T(8,128)(2,1)S(1)}, bf16[64,512]{1,0:T(8,128)(2,1)S(1)}, u32[]{:S(2)}, u32[]{:S(2)}) collective-permute-start(bf16[64,512]{1,0:T(8,128)(2,1)S(1)} %add_convert_fusion.3), channel_id=1, source_target_pairs={{0,24},{8,16},{16,8},{24,0},{32,56},{40,48},{48,40},{56,32},{64,88... | collective-permute-start | bytes 196616 | tf_op jit(solution)/shard_map/ppermute | solution.py:443
  110.0 6.9 %local_backward.3 = (bf16[2048,256]{1,0:T(8,128)(2,1)}, bf16[2048,256]{1,0:T(8,128)(2,1)}, bf16[2048,256]{1,0:T(8,128)(2,1)}) custom-call(bf16[2048,256]{1,0:T(8,128)(2,1)} %q_ref.9, bf16[2048,256]{1,0:T(8,128)(2,1)} %k_ref.9, bf16[2048,256]{1,0:T(8,128)(2,1)} %v_ref.9, ...), custom_call_target="tpu_custom_call", output_to_operand_aliasing={{0}: (9, {}), {1}: (10, {}), {2}: (11, {})} | custom-call | bytes 400000 | tf_op jit(solution)/shard_map/local_backward/pallas_call | solution.py:368
  117.4 4.3 %collective-permute-start.21 = (bf16[64,512]{1,0:T(8,128)(2,1)S(1)}, bf16[64,512]{1,0:T(8,128)(2,1)S(1)}, u32[]{:S(2)}, u32[]{:S(2)}) collective-permute-start(bf16[64,512]{1,0:T(8,128)(2,1)S(1)} %get-tuple-element.122), channel_id=1, source_target_pairs={{0,48},{8,56},{16,32},{24,40},{32,16},{40,24},{48,0},{56,8},{64,11... | collective-permute-start | bytes 196616 | tf_op jit(solution)/shard_map/ppermute | solution.py:443
  122.0 1.3 collective-permute-start.18
  123.9 2.5 %collective-permute-start.20 = (bf16[128,512]{1,0:T(8,128)(2,1)S(1)}, bf16[128,512]{1,0:T(8,128)(2,1)S(1)}, u32[]{:S(2)}, u32[]{:S(2)}) collective-permute-start(bf16[128,512]{1,0:T(8,128)(2,1)S(1)} %constant_dynamic-update-slice_fusion.34), channel_id=1, source_target_pairs={{0,24},{8,16},{16,8},{24,0},{32,56},{40,48},{48,40},{56,32},{64,88... | collective-permute-start | bytes 393224 | tf_op jit(solution)/shard_map/ppermute | solution.py:438
  127.0 6.7 %mix.1 = bf16[256,2048]{1,0:T(8,128)(2,1)} custom-call(bf16[8,256,256]{2,1,0:T(8,128)(2,1)} %copy-done.1, bf16[2048,2048]{1,0:T(8,128)(2,1)} %all-gather.5.cloned.1.call-done.w_ref), custom_call_target="tpu_custom_call" | custom-call | bytes 300000 | tf_op jit(solution)/shard_map/mix/pallas_call | solution.py:426
  133.8 1.9 %collective-permute-done.20.r3 = bf16[128,512]{1,0:T(8,128)(2,1)S(1)} collective-permute-done((bf16[128,512]{1,0:T(8,128)(2,1)S(1)}, bf16[128,512]{1,0:T(8,128)(2,1)S(1)}, u32[]{:S(2)}, u32[]{:S(2)}) %collective-permute-start.20) | collective-permute-done | bytes 131104 | tf_op jit(solution)/shard_map/ppermute | solution.py:438
  136.0 1.2 collective-permute-start.23
  137.2 0.9 collective-permute-start.24
  138.1 3.2 %finish.1 = (bf16[2048,256]{1,0:T(8,128)(2,1)}, bf16[2048,256]{1,0:T(8,128)(2,1)}) custom-call(bf16[2048,256]{1,0:T(8,128)(2,1)} %get-tuple-element.113.dk_ref, bf16[2048,256]{1,0:T(8,128)(2,1)} %get-tuple-element.114.dv_ref, bf16[64,512]{1,0:T(8,128)(2,1)} %pad_maximum_fusion.3.own, bf16[256,512]{1,0:T(8,128)(2,1)} %copy-done.4, ...), custom_call_target="tpu_custom_call" | custom-call | bytes 200000 | tf_op jit(solution)/shard_map/finish/pallas_call | solution.py:396
  141.5 1.0 collective-permute-done.23
  142.4 2.2 %collective-permute-done.24 = bf16[256,512]{1,0:T(8,128)(2,1)S(1)} collective-permute-done((bf16[256,512]{1,0:T(8,128)(2,1)S(1)}, bf16[256,512]{1,0:T(8,128)(2,1)S(1)}, u32[]{:S(2)}, u32[]{:S(2)}) %collective-permute-start.24) | collective-permute-done | bytes 262176 | tf_op jit(solution)/shard_map/ppermute | solution.py:448
  144.7 4.7 %collective-permute-start.25 = (bf16[128,512]{1,0:T(8,128)(2,1)S(1)}, bf16[128,512]{1,0:T(8,128)(2,1)S(1)}, u32[]{:S(2)}, u32[]{:S(2)}) collective-permute-start(bf16[128,512]{1,0:T(8,128)(2,1)S(1)} %slice.187), channel_id=1, source_target_pairs={{0,64},{8,72},{16,80},{24,88},{32,96},{40,104},{48,112},{56,120},{... | collective-permute-start | bytes 393224 | tf_op jit(solution)/shard_map/ppermute | solution.py:448
  149.6 2.3 %collective-permute-done.25 = bf16[128,512]{1,0:T(8,128)(2,1)S(1)} collective-permute-done((bf16[128,512]{1,0:T(8,128)(2,1)S(1)}, bf16[128,512]{1,0:T(8,128)(2,1)S(1)}, u32[]{:S(2)}, u32[]{:S(2)}) %collective-permute-start.25) | collective-permute-done | bytes 131104 | tf_op jit(solution)/shard_map/ppermute | solution.py:448
  151.9 2.5 %collective-permute-done.26 = bf16[128,512]{1,0:T(8,128)(2,1)S(1)} collective-permute-done((bf16[128,512]{1,0:T(8,128)(2,1)S(1)}, bf16[128,512]{1,0:T(8,128)(2,1)S(1)}, u32[]{:S(2)}, u32[]{:S(2)}) %collective-permute-start.26) | collective-permute-done | bytes 131104 | tf_op jit(solution)/shard_map/ppermute | solution.py:448
  154.5 1.0 copy-done.3
  (106 shorter events, 5.5 us)
Async XLA Ops:
  7.2 57.8 %all-gather.3.cloned.1.call-start = ((), (), s32[]{:S(2)}) async-start(), calls=%async_computation.1 | async-start | bytes 9437184 | tf_op jit(solution)/shard_map/all_gather | solution.py:487
  7.9 119.1 %all-gather.5.cloned.1.call-start = ((), (), s32[]{:S(2)}) async-start(), calls=%async_computation.2 | async-start | bytes 9437184 | tf_op jit(solution)/shard_map/all_gather | solution.py:488
  15.1 13.5 %collective-permute-start.1 = (bf16[128,512]{1,0:T(8,128)(2,1)}, bf16[128,512]{1,0:T(8,128)(2,1)S(1)}, u32[]{:S(2)}, u32[]{:S(2)}) collective-permute-start(bf16[128,512]{1,0:T(8,128)(2,1)} %get-tuple-element.71), channel_id=1, source_target_pairs={{0,16},{8,24},{16,0},{24,8},{32,48},{40,56},{48,32},{56,40},{64,80... | collective-permute-start | bytes 393224 | tf_op jit(solution)/shard_map/ppermute | solution.py:438
  18.3 10.2 %collective-permute-start.2 = (bf16[128,512]{1,0:T(8,128)(2,1)}, bf16[128,512]{1,0:T(8,128)(2,1)S(1)}, u32[]{:S(2)}, u32[]{:S(2)}) collective-permute-start(bf16[128,512]{1,0:T(8,128)(2,1)} %get-tuple-element.71), channel_id=1, source_target_pairs={{0,24},{8,16},{16,8},{24,0},{32,56},{40,48},{48,40},{56,32},{64,88... | collective-permute-start | bytes 393224 | tf_op jit(solution)/shard_map/ppermute | solution.py:438
  19.8 10.7 %collective-permute-start = (bf16[192,512]{1,0:T(8,128)(2,1)}, bf16[192,512]{1,0:T(8,128)(2,1)S(1)}, u32[]{:S(2)}, u32[]{:S(2)}) collective-permute-start(bf16[192,512]{1,0:T(8,128)(2,1)} %get-tuple-element.70), channel_id=1, source_target_pairs={{0,8},{8,0},{16,24},{24,16},{32,40},{40,32},{48,56},{56,48},{64,72... | collective-permute-start | bytes 589832 | tf_op jit(solution)/shard_map/ppermute | solution.py:438
  28.5 25.1 %copy-start.6 = (bf16[128,512]{1,0:T(8,128)(2,1)}, bf16[128,512]{1,0:T(8,128)(2,1)S(1)}, u32[]{:S(2)}) copy-start(bf16[128,512]{1,0:T(8,128)(2,1)S(1)} %collective-permute-done.1.refs_1_) | copy-start | bytes 393220
  28.5 25.0 %copy-start.7 = (bf16[128,512]{1,0:T(8,128)(2,1)}, bf16[128,512]{1,0:T(8,128)(2,1)S(1)}, u32[]{:S(2)}) copy-start(bf16[128,512]{1,0:T(8,128)(2,1)S(1)} %collective-permute-done.2.refs_2_) | copy-start | bytes 393220
  30.5 23.1 %copy-start.5 = (bf16[192,512]{1,0:T(8,128)(2,1)}, bf16[192,512]{1,0:T(8,128)(2,1)S(1)}, u32[]{:S(2)}) copy-start(bf16[192,512]{1,0:T(8,128)(2,1)S(1)} %collective-permute-done.refs_0_) | copy-start | bytes 589828
  31.3 17.2 %collective-permute-start.3 = (bf16[160,512]{1,0:T(8,128)(2,1)S(1)}, bf16[160,512]{1,0:T(8,128)(2,1)S(1)}, u32[]{:S(2)}, u32[]{:S(2)}) collective-permute-start(bf16[160,512]{1,0:T(8,128)(2,1)S(1)} %get-tuple-element.148), channel_id=1, source_target_pairs={{0,56},{8,48},{16,40},{24,32},{32,24},{40,16},{48,8},{56,0},{64,12... | collective-permute-start | bytes 491528 | tf_op jit(solution)/shard_map/ppermute | solution.py:438
  36.5 6.2 %collective-permute-start.4 = (bf16[96,512]{1,0:T(8,128)(2,1)S(1)}, bf16[96,512]{1,0:T(8,128)(2,1)S(1)}, u32[]{:S(2)}, u32[]{:S(2)}) collective-permute-start(bf16[96,512]{1,0:T(8,128)(2,1)S(1)} %get-tuple-element.147), channel_id=1, source_target_pairs={{0,64},{8,72},{16,80},{24,88},{32,96},{40,104},{48,112},{56,120},{... | collective-permute-start | bytes 294920 | tf_op jit(solution)/shard_map/ppermute | solution.py:438
  37.8 10.7 %collective-permute-start.5 = (bf16[96,512]{1,0:T(8,128)(2,1)S(1)}, bf16[96,512]{1,0:T(8,128)(2,1)S(1)}, u32[]{:S(2)}, u32[]{:S(2)}) collective-permute-start(bf16[96,512]{1,0:T(8,128)(2,1)S(1)} %get-tuple-element.147), channel_id=1, source_target_pairs={{0,120},{8,112},{16,104},{24,96},{32,88},{40,80},{48,72},{56,64},{... | collective-permute-start | bytes 294920 | tf_op jit(solution)/shard_map/ppermute | solution.py:438
  42.7 10.9 %copy-start.9 = (bf16[96,512]{1,0:T(8,128)(2,1)}, bf16[96,512]{1,0:T(8,128)(2,1)S(1)}, u32[]{:S(2)}) copy-start(bf16[96,512]{1,0:T(8,128)(2,1)S(1)} %collective-permute-done.4.refs_4_) | copy-start | bytes 294916
  48.5 5.1 %copy-start.10 = (bf16[96,512]{1,0:T(8,128)(2,1)}, bf16[96,512]{1,0:T(8,128)(2,1)S(1)}, u32[]{:S(2)}) copy-start(bf16[96,512]{1,0:T(8,128)(2,1)S(1)} %collective-permute-done.5.refs_5_) | copy-start | bytes 294916
  48.5 5.1 %copy-start.8 = (bf16[160,512]{1,0:T(8,128)(2,1)}, bf16[160,512]{1,0:T(8,128)(2,1)S(1)}, u32[]{:S(2)}) copy-start(bf16[160,512]{1,0:T(8,128)(2,1)S(1)} %collective-permute-done.3.refs_3_) | copy-start | bytes 491524
  48.5 5.1 %collective-permute-start.6 = (bf16[128,512]{1,0:T(8,128)(2,1)S(1)}, bf16[128,512]{1,0:T(8,128)(2,1)S(1)}, u32[]{:S(2)}, u32[]{:S(2)}) collective-permute-start(bf16[128,512]{1,0:T(8,128)(2,1)S(1)} %constant_dynamic-update-slice_fusion.16), channel_id=1, source_target_pairs={{0,192},{8,200},{16,208},{24,216},{32,224},{40,232},{48,240},{56,2... | collective-permute-start | bytes 393224 | tf_op jit(solution)/shard_map/ppermute | solution.py:438
  53.6 0.6 copy-start.11
  60.2 33.3 %all-to-all-start = ((bf16[8,256,256]{2,1,0:T(8,128)(2,1)}), bf16[8,256,256]{2,1,0:T(8,128)(2,1)S(1)}, u32[]{:S(2)}, u32[]{:S(2)}) async-start(bf16[8,256,256]{2,1,0:T(8,128)(2,1)} %bitcast.7), calls=%async_computation | async-start | bytes 2097152 | tf_op jit(solution)/shard_map/all_to_all | solution.py:503
  64.5 10.3 %copy-start.2 = (bf16[256,2048]{1,0:T(8,128)(2,1)S(1)}, bf16[256,2048]{1,0:T(8,128)(2,1)}, u32[]{:S(2)}) copy-start(bf16[256,2048]{1,0:T(8,128)(2,1)} %param.8) | copy-start | bytes 3145732
  64.9 9.9 %copy-start = (bf16[2048,2048]{1,0:T(8,128)(2,1)S(1)}, bf16[2048,2048]{1,0:T(8,128)(2,1)}, u32[]{:S(2)}) copy-start(bf16[2048,2048]{1,0:T(8,128)(2,1)} %all-gather.3.cloned.1.call-done) | copy-start | bytes 25165828
  71.2 14.4 %collective-permute-start.7 = (bf16[256,512]{1,0:T(8,128)(2,1)S(1)}, bf16[256,512]{1,0:T(8,128)(2,1)S(1)}, u32[]{:S(2)}, u32[]{:S(2)}) collective-permute-start(bf16[256,512]{1,0:T(8,128)(2,1)S(1)} %get-tuple-element.125), channel_id=1, source_target_pairs={{0,64},{8,72},{16,80},{24,88},{32,96},{40,104},{48,112},{56,120},{... | collective-permute-start | bytes 786440 | tf_op jit(solution)/shard_map/ppermute | solution.py:438
  72.9 12.8 %collective-permute-start.8 = (bf16[256,512]{1,0:T(8,128)(2,1)S(1)}, bf16[256,512]{1,0:T(8,128)(2,1)S(1)}, u32[]{:S(2)}, u32[]{:S(2)}) collective-permute-start(bf16[256,512]{1,0:T(8,128)(2,1)S(1)} %get-tuple-element.124), channel_id=1, source_target_pairs={{0,128},{8,136},{16,144},{24,152},{32,160},{40,168},{48,176},{56,1... | collective-permute-start | bytes 786440 | tf_op jit(solution)/shard_map/ppermute | solution.py:438
  73.3 14.0 %collective-permute-start.9 = (bf16[256,512]{1,0:T(8,128)(2,1)S(1)}, bf16[256,512]{1,0:T(8,128)(2,1)S(1)}, u32[]{:S(2)}, u32[]{:S(2)}) collective-permute-start(bf16[256,512]{1,0:T(8,128)(2,1)S(1)} %get-tuple-element.123), channel_id=1, source_target_pairs={{0,192},{8,200},{16,208},{24,216},{32,224},{40,232},{48,240},{56,2... | collective-permute-start | bytes 786440 | tf_op jit(solution)/shard_map/ppermute | solution.py:438
  84.1 22.3 %copy-start.13 = (bf16[128,512]{1,0:T(8,128)(2,1)S(1)}, bf16[128,512]{1,0:T(8,128)(2,1)}, u32[]{:S(2)}) copy-start(bf16[128,512]{1,0:T(8,128)(2,1)} %get-tuple-element.95) | copy-start | bytes 393220
  84.1 25.9 %copy-start.12 = (bf16[128,512]{1,0:T(8,128)(2,1)S(1)}, bf16[128,512]{1,0:T(8,128)(2,1)}, u32[]{:S(2)}) copy-start(bf16[128,512]{1,0:T(8,128)(2,1)} %get-tuple-element.108) | copy-start | bytes 393220
  84.1 16.8 %collective-permute-start.13 = (bf16[128,512]{1,0:T(8,128)(2,1)}, bf16[128,512]{1,0:T(8,128)(2,1)S(1)}, u32[]{:S(2)}, u32[]{:S(2)}) collective-permute-start(bf16[128,512]{1,0:T(8,128)(2,1)} %get-tuple-element.87), channel_id=1, source_target_pairs={{0,192},{8,200},{16,208},{24,216},{32,224},{40,232},{48,240},{56,2... | collective-permute-start | bytes 393224 | tf_op jit(solution)/shard_map/ppermute | solution.py:438
  87.5 13.4 %collective-permute-start.10 = (bf16[64,512]{1,0:T(8,128)(2,1)S(1)}, bf16[64,512]{1,0:T(8,128)(2,1)S(1)}, u32[]{:S(2)}, u32[]{:S(2)}) collective-permute-start(bf16[64,512]{1,0:T(8,128)(2,1)S(1)} %get-tuple-element.128), channel_id=1, source_target_pairs={{0,8},{8,0},{16,24},{24,16},{32,40},{40,32},{48,56},{56,48},{64,72... | collective-permute-start | bytes 196616 | tf_op jit(solution)/shard_map/ppermute | solution.py:443
  89.0 11.9 %collective-permute-start.11 = (bf16[64,512]{1,0:T(8,128)(2,1)S(1)}, bf16[64,512]{1,0:T(8,128)(2,1)S(1)}, u32[]{:S(2)}, u32[]{:S(2)}) collective-permute-start(bf16[64,512]{1,0:T(8,128)(2,1)S(1)} %get-tuple-element.127), channel_id=1, source_target_pairs={{0,48},{8,56},{16,32},{24,40},{32,16},{40,24},{48,0},{56,8},{64,11... | collective-permute-start | bytes 196616 | tf_op jit(solution)/shard_map/ppermute | solution.py:443
  92.6 8.3 %collective-permute-start.12 = (bf16[64,512]{1,0:T(8,128)(2,1)S(1)}, bf16[64,512]{1,0:T(8,128)(2,1)S(1)}, u32[]{:S(2)}, u32[]{:S(2)}) collective-permute-start(bf16[64,512]{1,0:T(8,128)(2,1)S(1)} %get-tuple-element.126), channel_id=1, source_target_pairs={{0,56},{8,48},{16,40},{24,32},{32,24},{40,16},{48,8},{56,0},{64,12... | collective-permute-start | bytes 196616 | tf_op jit(solution)/shard_map/ppermute | solution.py:443
  93.5 23.4 %copy-start.1 = (bf16[8,256,256]{2,1,0:T(8,128)(2,1)}, bf16[8,256,256]{2,1,0:T(8,128)(2,1)S(1)}, u32[]{:S(2)}) copy-start(bf16[8,256,256]{2,1,0:T(8,128)(2,1)S(1)} %all-to-all-done.att_ref) | copy-start | bytes 3145732
  101.0 16.0 %collective-permute-start.17 = (bf16[96,512]{1,0:T(8,128)(2,1)S(1)}, bf16[96,512]{1,0:T(8,128)(2,1)S(1)}, u32[]{:S(2)}, u32[]{:S(2)}) collective-permute-start(bf16[96,512]{1,0:T(8,128)(2,1)S(1)} %pad_maximum_fusion.2), channel_id=1, source_target_pairs={{0,120},{8,112},{16,104},{24,96},{32,88},{40,80},{48,72},{56,64},{... | collective-permute-start | bytes 294920 | tf_op jit(solution)/shard_map/ppermute | solution.py:438
  106.3 10.7 %collective-permute-start.16 = (bf16[96,512]{1,0:T(8,128)(2,1)S(1)}, bf16[96,512]{1,0:T(8,128)(2,1)S(1)}, u32[]{:S(2)}, u32[]{:S(2)}) collective-permute-start(bf16[96,512]{1,0:T(8,128)(2,1)S(1)} %pad_maximum_fusion.1), channel_id=1, source_target_pairs={{0,64},{8,72},{16,80},{24,88},{32,96},{40,104},{48,112},{56,120},{... | collective-permute-start | bytes 294920 | tf_op jit(solution)/shard_map/ppermute | solution.py:438
  106.4 10.9 %collective-permute-start.15 = (bf16[160,512]{1,0:T(8,128)(2,1)S(1)}, bf16[160,512]{1,0:T(8,128)(2,1)S(1)}, u32[]{:S(2)}, u32[]{:S(2)}) collective-permute-start(bf16[160,512]{1,0:T(8,128)(2,1)S(1)} %pad_maximum_fusion), channel_id=1, source_target_pairs={{0,56},{8,48},{16,40},{24,32},{32,24},{40,16},{48,8},{56,0},{64,12... | collective-permute-start | bytes 491528 | tf_op jit(solution)/shard_map/ppermute | solution.py:438
  107.1 9.9 %collective-permute-start.14 = (bf16[64,512]{1,0:T(8,128)(2,1)S(1)}, bf16[64,512]{1,0:T(8,128)(2,1)S(1)}, u32[]{:S(2)}, u32[]{:S(2)}) collective-permute-start(bf16[64,512]{1,0:T(8,128)(2,1)S(1)} %add_convert_fusion.3), channel_id=1, source_target_pairs={{0,24},{8,16},{16,8},{24,0},{32,56},{40,48},{48,40},{56,32},{64,88... | collective-permute-start | bytes 196616 | tf_op jit(solution)/shard_map/ppermute | solution.py:443
  117.4 16.4 %collective-permute-start.21 = (bf16[64,512]{1,0:T(8,128)(2,1)S(1)}, bf16[64,512]{1,0:T(8,128)(2,1)S(1)}, u32[]{:S(2)}, u32[]{:S(2)}) collective-permute-start(bf16[64,512]{1,0:T(8,128)(2,1)S(1)} %get-tuple-element.122), channel_id=1, source_target_pairs={{0,48},{8,56},{16,32},{24,40},{32,16},{40,24},{48,0},{56,8},{64,11... | collective-permute-start | bytes 196616 | tf_op jit(solution)/shard_map/ppermute | solution.py:443
  121.7 12.0 %collective-permute-start.22 = (bf16[64,512]{1,0:T(8,128)(2,1)S(1)}, bf16[64,512]{1,0:T(8,128)(2,1)S(1)}, u32[]{:S(2)}, u32[]{:S(2)}) collective-permute-start(bf16[64,512]{1,0:T(8,128)(2,1)S(1)} %get-tuple-element.122), channel_id=1, source_target_pairs={{0,56},{8,48},{16,40},{24,32},{32,24},{40,16},{48,8},{56,0},{64,12... | collective-permute-start | bytes 196616 | tf_op jit(solution)/shard_map/ppermute | solution.py:443
  122.0 13.9 %collective-permute-start.18 = (bf16[256,512]{1,0:T(8,128)(2,1)S(1)}, bf16[256,512]{1,0:T(8,128)(2,1)S(1)}, u32[]{:S(2)}, u32[]{:S(2)}) collective-permute-start(bf16[256,512]{1,0:T(8,128)(2,1)S(1)} %get-tuple-element.121), channel_id=1, source_target_pairs={{0,8},{8,0},{16,24},{24,16},{32,40},{40,32},{48,56},{56,48},{64,72... | collective-permute-start | bytes 786440 | tf_op jit(solution)/shard_map/ppermute | solution.py:438
  123.3 10.5 %collective-permute-start.19 = (bf16[128,512]{1,0:T(8,128)(2,1)S(1)}, bf16[128,512]{1,0:T(8,128)(2,1)S(1)}, u32[]{:S(2)}, u32[]{:S(2)}) collective-permute-start(bf16[128,512]{1,0:T(8,128)(2,1)S(1)} %constant_dynamic-update-slice_fusion.29), channel_id=1, source_target_pairs={{0,16},{8,24},{16,0},{24,8},{32,48},{40,56},{48,32},{56,40},{64,80... | collective-permute-start | bytes 393224 | tf_op jit(solution)/shard_map/ppermute | solution.py:438
  123.9 11.7 %collective-permute-start.20 = (bf16[128,512]{1,0:T(8,128)(2,1)S(1)}, bf16[128,512]{1,0:T(8,128)(2,1)S(1)}, u32[]{:S(2)}, u32[]{:S(2)}) collective-permute-start(bf16[128,512]{1,0:T(8,128)(2,1)S(1)} %constant_dynamic-update-slice_fusion.34), channel_id=1, source_target_pairs={{0,24},{8,16},{16,8},{24,0},{32,56},{40,48},{48,40},{56,32},{64,88... | collective-permute-start | bytes 393224 | tf_op jit(solution)/shard_map/ppermute | solution.py:438
  133.8 4.3 %copy-start.14 = (bf16[128,512]{1,0:T(8,128)(2,1)}, bf16[128,512]{1,0:T(8,128)(2,1)S(1)}, u32[]{:S(2)}) copy-start(bf16[128,512]{1,0:T(8,128)(2,1)S(1)} %collective-permute-done.19.r2) | copy-start | bytes 393220
  135.6 2.5 %copy-start.15 = (bf16[128,512]{1,0:T(8,128)(2,1)}, bf16[128,512]{1,0:T(8,128)(2,1)S(1)}, u32[]{:S(2)}) copy-start(bf16[128,512]{1,0:T(8,128)(2,1)S(1)} %collective-permute-done.20.r3) | copy-start | bytes 393220
  135.9 2.2 %copy-start.4 = (bf16[256,512]{1,0:T(8,128)(2,1)}, bf16[256,512]{1,0:T(8,128)(2,1)S(1)}, u32[]{:S(2)}) copy-start(bf16[256,512]{1,0:T(8,128)(2,1)S(1)} %collective-permute-done.18.r1) | copy-start | bytes 786436
  136.0 6.5 %collective-permute-start.23 = (bf16[256,512]{1,0:T(8,128)(2,1)S(1)}, bf16[256,512]{1,0:T(8,128)(2,1)S(1)}, u32[]{:S(2)}, u32[]{:S(2)}) collective-permute-start(bf16[256,512]{1,0:T(8,128)(2,1)S(1)} %constant_dynamic-update-slice_fusion.42), channel_id=1, source_target_pairs={{0,64},{8,72},{16,80},{24,88},{32,96},{40,104},{48,112},{56,120},{... | collective-permute-start | bytes 786440 | tf_op jit(solution)/shard_map/ppermute | solution.py:448
  137.2 7.5 %collective-permute-start.24 = (bf16[256,512]{1,0:T(8,128)(2,1)S(1)}, bf16[256,512]{1,0:T(8,128)(2,1)S(1)}, u32[]{:S(2)}, u32[]{:S(2)}) collective-permute-start(bf16[256,512]{1,0:T(8,128)(2,1)S(1)} %constant_dynamic-update-slice_fusion.42), channel_id=1, source_target_pairs={{0,192},{8,200},{16,208},{24,216},{32,224},{40,232},{48,240},{56,2... | collective-permute-start | bytes 786440 | tf_op jit(solution)/shard_map/ppermute | solution.py:448
  144.7 7.2 %collective-permute-start.25 = (bf16[128,512]{1,0:T(8,128)(2,1)S(1)}, bf16[128,512]{1,0:T(8,128)(2,1)S(1)}, u32[]{:S(2)}, u32[]{:S(2)}) collective-permute-start(bf16[128,512]{1,0:T(8,128)(2,1)S(1)} %slice.187), channel_id=1, source_target_pairs={{0,64},{8,72},{16,80},{24,88},{32,96},{40,104},{48,112},{56,120},{... | collective-permute-start | bytes 393224 | tf_op jit(solution)/shard_map/ppermute | solution.py:448
  149.4 5.0 %collective-permute-start.26 = (bf16[128,512]{1,0:T(8,128)(2,1)S(1)}, bf16[128,512]{1,0:T(8,128)(2,1)S(1)}, u32[]{:S(2)}, u32[]{:S(2)}) collective-permute-start(bf16[128,512]{1,0:T(8,128)(2,1)S(1)} %slice.188), channel_id=1, source_target_pairs={{0,192},{8,200},{16,208},{24,216},{32,224},{40,232},{48,240},{56,2... | collective-permute-start | bytes 393224 | tf_op jit(solution)/shard_map/ppermute | solution.py:448
  154.5 1.0 copy-start.3
Sparse Core Ops, SparseCore 0:
  9.9 55.0 all-gather.2
  66.8 52.4 all-gather.4
where the time goes:
time: 163 us; the launch traced here: 162 us
  Pallas kernels  51.6 us (32%)
  starting transfers between devices  50.6 us (31%)
  waiting for transfers between devices  29 us (18%)
  between operations  14.6 us (9%)
  matrix products  9.55 us (6%)
  local copies, waits for them, and re-layouts  6.08 us (4%)
    ppermute x17, starting transfers between devices, swap(): lax.ppermute(x, axis, [(i, i ^ distance) for i in range(lax.axis_size(axi...  26.7 us
    ppermute x17, waiting for transfers between devices, swap(): lax.ppermute(x, axis, [(i, i ^ distance) for i in range(lax.axis_size(axi...  19.1 us
    pallas_call x2, Pallas kernels, local_backward(): call(local_backward_kernel, 8, grid=(1,), in_specs=[columns] * 6 + [wide]...  14.3 us
    ppermute x6, starting transfers between devices, swap_z(): lax.ppermute(x, 'seq', [(i, place(i)) for i in range(lax.axis_size('seq'))])  12.7 us
    pallas_call x2, Pallas kernels, local_forward(): call(local_forward_kernel, 5, grid=(1,), in_specs=[columns] * 6, out_spec...  9.06 us
    ppermute x4, waiting for transfers between devices, shift_y(): lax.ppermute(x, 'seq', [(i, (i + 8 * distance) % n) for i in range(n)])  8.09 us
    ppermute x4, starting transfers between devices, shift_y(): lax.ppermute(x, 'seq', [(i, (i + 8 * distance) % n) for i in range(n)])  6.9 us
    pallas_call x1, Pallas kernels, mix(): call(mix_kernel, 6, in_specs=[whole, pl.BlockSpec(memory_space=pl.ANY)],...  6.66 us
  transfers between devices with their start and end apart: 30, of which 13 were waited for; matrix products, arithmetic and copies ran while one was open for 9% of the time, Pallas kernels for 32%

commit v1 on v0

--- a/solution.py
+++ b/solution.py
@@ -378,12 +378,12 @@
     )(*inputs, *before)
 
 
-def finish_kernel(dk_ref, dv_ref, own, r1, r2, r3, gk_ref, gv_ref, small):
+def finish_kernel(dk_ref, dv_ref, own, across, r1, r2, r3, gk_ref, gv_ref, small):
     rows = lambda ref, lo, hi: ref[lo:hi, :].astype(F32)
     x4 = rows(r1, 0, 128)
     x5 = rows(r2, 0, 64) + rows(r3, 0, 64)
-    rest = rows(own, 0, 64) + rows(r1, 128, 192) + rows(r2, 64, 128) + rows(r3, 64, 128)
-    packed = jnp.concatenate([x4, x5, rest], axis=0)
+    own, across = rows(own, 0, 64), rows(across, 0, 32)
+    packed = jnp.concatenate([x4, x5, own[:32], across[8:24], own[32:40] + across[24:]], axis=0)
     parts = [spread_levels(packed[:, half], small, 1.0) for half in (slice(0, HD), slice(HD, None))]
     for at, x in repeat16(jnp.concatenate(parts, axis=1)):
         gk_ref[at, :] = (dk_ref[at, :].astype(F32) + x[:, :HD]).astype(BF16)
@@ -397,7 +397,7 @@
         finish_kernel,
         4,
         grid=(width // HD,),
-        in_specs=[spec(tokens)] * 2 + [both(n) for n in (64, 256, 128, 128)],
+        in_specs=[spec(tokens)] * 2 + [both(n) for n in (64, 32, 192, 128, 128)],
         out_specs=[spec(tokens)] * 2,
         out_shape=[shape] * 2,
         scratch_shapes=[pltpu.VMEM((B, HD), F32)],
@@ -438,11 +438,6 @@
     return lax.ppermute(x, axis, [(i, i ^ distance) for i in range(lax.axis_size(axis))])
 
 
-def swap_z(x, distance):
-    place = lambda i: (i & 24) | ((((i - 2) & 7) ^ distance) + 2) & 7
-    return lax.ppermute(x, "seq", [(i, place(i)) for i in range(lax.axis_size("seq"))])
-
-
 def shift_y(x, distance):
     n = lax.axis_size("seq")
     return lax.ppermute(x, "seq", [(i, (i + 8 * distance) % n) for i in range(n)])
@@ -465,16 +460,16 @@
     return sum(x.astype(F32) for x in parts).astype(BF16)
 
 
-def quarters(x, place, axis):
-    n = x.shape[axis] // 4
-    return [lax.dynamic_slice_in_dim(x, (place ^ j) * n, n, axis) for j in range(4)]
-
-
-def join_quarters(parts, places, axis):
-    n = parts[0].shape[axis]
-    whole = jnp.concatenate([jnp.zeros(p.shape, p.dtype) for p in parts], axis)
+def quarters(x, place):
+    n = x.shape[1] // 4
+    return [lax.dynamic_slice_in_dim(x, (place ^ j) * n, n, 1) for j in range(4)]
+
+
+def join_quarters(parts, places):
+    n = parts[0].shape[1]
+    whole = jnp.concatenate([jnp.zeros(p.shape, p.dtype) for p in parts], 1)
     for place, part in zip(places, parts):
-        whole = lax.dynamic_update_slice_in_dim(whole, part, place * n, axis)
+        whole = lax.dynamic_update_slice_in_dim(whole, part, place * n, 1)
     return whole
 
 
@@ -482,8 +477,7 @@
     tokens, width = queries.shape
     shards = lax.axis_size("head")
     assert shards == 8 and lax.axis_size("seq") == 32
-    y, z = lax.axis_index("seq") >> 3, (lax.axis_index("seq") - 2) & 7
-    z = (z & 3) ^ (3 * (z >> 2))
+    y = lax.axis_index("seq") >> 3
     cotangent = lax.all_gather(grad_out, "head", axis=0, tiled=True)
     w_full = lax.all_gather(w_out, "head", axis=0, tiled=True)
 
@@ -503,47 +497,47 @@
     mine = lax.all_to_all(attended.reshape(shards, tokens // shards, width), "head", 0, 0)
     grad_weight = tn(attended, cotangent).astype(BF16)
     ga = nt(cotangent, after(w_out, grad_weight)).astype(BF16)
-    own, *rest = quarters(grad_weight, y, 1)
+    own, *rest = quarters(grad_weight, y)
     rest = [swap(x, "seq", 8 * (j + 1)) for j, x in enumerate(rest)]
     g0, gc, dq4, e4, e5, e6, e7, e8 = coarse_backward(ga, attended, rtot, qc, side)
     rest = after(tuple(rest), dq4)
     partial = add(own, *rest)
     mine = after(mine, dq4)
 
-    x8 = swap(e8, "seq", 24)
-    own, *rest = quarters(partial, z, 0)
-    rest = [swap_z(x, j + 1) for j, x in enumerate(rest)]
+    x8 = swap(after(e8, mine), "seq", 24)
+    low = swap(partial, "seq", 1)
     inputs = (queries, keys, values, qc, kc, vc, g0, gc)
     done = local_backward(0, inputs + (after(dq4, partial),))
-    rest, x8 = after((rest, x8), done[0])
-    partial = add(own, *rest)
-
-    f7 = swap(cat([e6, x8[32:64]]), "seq", 7)
-    f8 = swap(cat([e7[:64], x8[64:96]]), "seq", 8)
-    f15 = swap(cat([e7[64:], x8[96:]]), "seq", 15)
-    low = swap_z(partial, 7)
+    low, x8 = after((low, x8), done[0])
+    partial = add(partial, low)
+
+    f7 = swap(cat([e6, e7[64:], x8[32:64], x8[96:]]), "seq", 7)
+    low = swap(partial, "seq", 3)
     grad_q, dk, dv = local_backward(1, inputs + (after(dq4, partial, x8),), done)
-    low, f7, f8, f15 = after((low, f7, f8, f15), grad_q)
+    low, f7 = after((low, f7), grad_q)
     partial = add(partial, low)
 
-    x6, x7, x8 = f7[:B], add(f8[:64], f15[:64]), add(x8[:32], f7[B:], f8[64:], f15[64:])
+    x6, x7 = f7[:B], add(e7[:64], f7[128:192])
+    here, there = add(x8[:32], f7[192:224]), add(x8[64:96], f7[224:])
     first = [e4, e5[:64], e5[64:]]
-    pad = jnp.zeros((8, x8.shape[1]), BF16)
-    tails = [cat([x6[32 * j:][:32], x7[16 * j:][:16], x8[8 * j:][:8], pad]) for j in range(4)]
-    messages = [[x, tails[j + 1]] for j, x in enumerate(first)]
-    messages[0].append(partial)
-    near = [swap(cat(x), "seq", j + 1) for j, x in enumerate(messages)]
-    rest = [swap_z(partial, j) for j in (2, 3)]
+    tails = []
+    for j in range(4):
+        tails.append(cat([x6[32 * j:][:32], here[8 * j:][:8], x7[16 * j:][:16], there[8 * j:][:8]]))
+    near = [swap(cat([x, tails[j + 1]]), "seq", j + 1) for j, x in enumerate(first)]
+    low = swap(partial, "seq", 7)
     mixed = mix(after(mine, partial, tails[0]), w_full)
-    near, rest = after((near, rest), mixed)
-    summed = join_quarters([partial, near[0][192:]] + rest, [z ^ j for j in range(4)], 0)
-
+    near, low = after((near, low), mixed)
+    summed = add(partial, low)
+
+    tail = add(tails[0], *[x[x.shape[0] - 64:] for x in near])
+    across = swap(tail[32:], "seq", 8)
     up, down = shift_y(summed, 1), shift_y(summed, -1)
-    grad_k, grad_v = finish(after(dk, summed), dv, (tails[0], *near))
-    up, down = after((up, down), grad_k)
+    up, down, across = after((up, down, across), summed)
     far = cat([shift_y(up[:B], 1), shift_y(down[B:], -1)])
+    grad_k, grad_v = finish(after(dk, up, down), dv, (tail, across, *near))
+    far = after(far, grad_k)
     places = [y, (y + 3) & 3, (y + 1) & 3, (y + 2) & 3]
-    return mixed, grad_q, grad_k, grad_v, join_quarters([summed, up, down, far], places, 1)
+    return mixed, grad_q, grad_k, grad_v, join_quarters([summed, up, down, far], places)
 
 
 def solution(mesh):

time: 163 us -> 160 us (0.982)
  starting transfers between devices: 50.6 us -> 42.4 us
  waiting for transfers between devices: 29 us -> 35.5 us
    ppermute x17 -> x19, waiting for transfers between devices: 19.1 us -> 33.1 us  [swap(): lax.ppermute(x, axis, [(i, i ^ distance) for i in range(lax.axis_size(axi...]
    ppermute x6 -> x0, starting transfers between devices: 12.7 us -> none  [swap_z(): lax.ppermute(x, 'seq', [(i, place(i)) for i in range(lax.axis_size('seq'))])]
    ppermute x4, waiting for transfers between devices: 8.09 us -> 0.64 us  [shift_y(): lax.ppermute(x, 'seq', [(i, (i + 8 * distance) % n) for i in range(n)])]
    ppermute x17 -> x19, starting transfers between devices: 26.7 us -> 31.9 us  [swap(): lax.ppermute(x, axis, [(i, i ^ distance) for i in range(lax.axis_size(axi...]
    unnamed x52 -> x56, local copies, waits for them, and re-layouts: 4.8 us -> 3.92 us
  transfers between devices with their start and end apart: 30 -> 26, of which waited for: 13 -> 12; matrix products, arithmetic and copies ran while one was open for 9% -> 8% of each run, Pallas kernels for 32% -> 32%
where the time goes in v1:
time: 160 us; the launch traced here: 159 us
  Pallas kernels  51.3 us (32%)
  starting transfers between devices  42.4 us (26%)
  waiting for transfers between devices  35.5 us (22%)
  between operations  14.5 us (9%)
  matrix products  9.55 us (6%)
  local copies, waits for them, and re-layouts  5.13 us (3%)
    ppermute x19, waiting for transfers between devices, swap(): lax.ppermute(x, axis, [(i, i ^ distance) for i in range(lax.axis_size(axi...  33.1 us
    ppermute x19, starting transfers between devices, swap(): lax.ppermute(x, axis, [(i, i ^ distance) for i in range(lax.axis_size(axi...  31.9 us
    pallas_call x2, Pallas kernels, local_backward(): call(local_backward_kernel, 8, grid=(1,), in_specs=[columns] * 6 + [wide]...  14.1 us
    pallas_call x2, Pallas kernels, local_forward(): call(local_forward_kernel, 5, grid=(1,), in_specs=[columns] * 6, out_spec...  9.06 us
    pallas_call x1, Pallas kernels, mix(): call(mix_kernel, 6, in_specs=[whole, pl.BlockSpec(memory_space=pl.ANY)],...  6.66 us
    pallas_call x1, Pallas kernels, coarsen(): call(coarsen_kernel, 6, grid=(width // HD,), in_specs=[spec(tokens)] * 3,...  6.41 us
    dot_general x1, matrix products, tn(): lax.dot_general(a, b, (((0,), (0,)), ((), ())), preferred_element_type=F32)  6.19 us
    ppermute x4, starting transfers between devices, shift_y(): lax.ppermute(x, 'seq', [(i, (i + 8 * distance) % n) for i in range(n)])  6.16 us
  transfers between devices with their start and end apart: 26, of which 12 were waited for; matrix products, arithmetic and copies ran while one was open for 8% of the time, Pallas kernels for 32%

profile of v1, /device:TPU:16, one launch (start us, length us, event | category | flops | bytes accessed | tf_op | source)
XLA Modules:
  0.0 158.9 jit_solution(16545100074658038596)
XLA Ops:
  7.2 0.7 all-gather.3.cloned.1.call-update
  7.9 0.7 all-gather.5.cloned.1.call-update
  8.6 6.4 %coarsen.1 = (bf16[2048,256]{1,0:T(8,128)(2,1)}, bf16[2048,256]{1,0:T(8,128)(2,1)}, bf16[2048,256]{1,0:T(8,128)(2,1)}, bf16[192,512]{1,0:T(8,128)(2,1)}, bf16[128,512]{1,0:T(8,128)(2,1)}) custom-call(bf16[2048,256]{1,0:T(8,128)(2,1)} %q_ref.9, bf16[2048,256]{1,0:T(8,128)(2,1)} %k_ref.9, bf16[2048,256]{1,0:T(8,128)(2,1)} %v_ref.9), custom_call_target="tpu_custom_call" | custom-call | bytes 300000 | tf_op jit(solution)/shard_map/coarsen/pallas_call | solution.py:106
  15.1 3.3 %collective-permute-start.1 = (bf16[128,512]{1,0:T(8,128)(2,1)}, bf16[128,512]{1,0:T(8,128)(2,1)S(1)}, u32[]{:S(2)}, u32[]{:S(2)}) collective-permute-start(bf16[128,512]{1,0:T(8,128)(2,1)} %get-tuple-element.69), channel_id=1, source_target_pairs={{0,16},{8,24},{16,0},{24,8},{32,48},{40,56},{48,32},{56,40},{64,80... | collective-permute-start | bytes 393224 | tf_op jit(solution)/shard_map/ppermute | solution.py:438
  18.3 1.4 collective-permute-start.2
  20.3 4.4 %local_forward.2 = (f32[1,2048,128]{2,1,0:T(8,128)}, f32[1,2048,128]{2,1,0:T(8,128)}) custom-call(bf16[2048,256]{1,0:T(8,128)(2,1)} %q_ref.9, bf16[2048,256]{1,0:T(8,128)(2,1)} %k_ref.9, bf16[2048,256]{1,0:T(8,128)(2,1)} %v_ref.9, bf16[2048,256]{1,0:T(8,128)(2,1)} %get-tuple-element.61.qc_ref.q_ref, bf16[2048,256]{1,0:T(8,128)(2,1)} %get-tuple-element.62.kc_ref, ...), custom_call_target="tpu_custom_call" | custom-call | bytes 250000 | tf_op jit(solution)/shard_map/local_forward/pallas_call | solution.py:160
  24.7 0.8 constant_dynamic-update-slice_fusion.7
  25.5 0.7 constant_dynamic-update-slice_fusion.15
  26.2 2.3 %collective-permute-done.1.refs_1_ = bf16[128,512]{1,0:T(8,128)(2,1)S(1)} collective-permute-done((bf16[128,512]{1,0:T(8,128)(2,1)}, bf16[128,512]{1,0:T(8,128)(2,1)S(1)}, u32[]{:S(2)}, u32[]{:S(2)}) %collective-permute-start.1) | collective-permute-done | bytes 131104 | tf_op jit(solution)/shard_map/ppermute | solution.py:438
  28.5 2.0 %collective-permute-done.refs_0_ = bf16[192,512]{1,0:T(8,128)(2,1)S(1)} collective-permute-done((bf16[192,512]{1,0:T(8,128)(2,1)}, bf16[192,512]{1,0:T(8,128)(2,1)S(1)}, u32[]{:S(2)}, u32[]{:S(2)}) %collective-permute-start) | collective-permute-done | bytes 196640 | tf_op jit(solution)/shard_map/ppermute | solution.py:438
  30.6 0.7 constant_dynamic-update-slice_fusion.22
  31.3 5.2 %collective-permute-start.3 = (bf16[160,512]{1,0:T(8,128)(2,1)S(1)}, bf16[160,512]{1,0:T(8,128)(2,1)S(1)}, u32[]{:S(2)}, u32[]{:S(2)}) collective-permute-start(bf16[160,512]{1,0:T(8,128)(2,1)S(1)} %get-tuple-element.140), channel_id=1, source_target_pairs={{0,56},{8,48},{16,40},{24,32},{32,24},{40,16},{48,8},{56,0},{64,12... | collective-permute-start | bytes 491528 | tf_op jit(solution)/shard_map/ppermute | solution.py:438
  36.5 1.3 collective-permute-start.4
  38.1 4.6 %local_forward.3 = (f32[1,2048,128]{2,1,0:T(8,128)}, f32[1,2048,128]{2,1,0:T(8,128)}) custom-call(bf16[2048,256]{1,0:T(8,128)(2,1)} %q_ref.9, bf16[2048,256]{1,0:T(8,128)(2,1)} %k_ref.9, bf16[2048,256]{1,0:T(8,128)(2,1)} %v_ref.9, bf16[2048,256]{1,0:T(8,128)(2,1)} %get-tuple-element.61.qc_ref.q_ref, bf16[2048,256]{1,0:T(8,128)(2,1)} %get-tuple-element.62.kc_ref, ...), custom_call_target="tpu_custom_call" | custom-call | bytes 250000 | tf_op jit(solution)/shard_map/local_forward/pallas_call | solution.py:160
  42.7 5.8 %collective-permute-done.5.refs_5_ = bf16[96,512]{1,0:T(8,128)(2,1)S(1)} collective-permute-done((bf16[96,512]{1,0:T(8,128)(2,1)S(1)}, bf16[96,512]{1,0:T(8,128)(2,1)S(1)}, u32[]{:S(2)}, u32[]{:S(2)}) %collective-permute-start.5) | collective-permute-done | bytes 98336 | tf_op jit(solution)/shard_map/ppermute | solution.py:438
  48.6 4.9 %collective-permute-done.6.refs_6_ = bf16[128,512]{1,0:T(8,128)(2,1)S(1)} collective-permute-done((bf16[128,512]{1,0:T(8,128)(2,1)S(1)}, bf16[128,512]{1,0:T(8,128)(2,1)S(1)}, u32[]{:S(2)}, u32[]{:S(2)}) %collective-permute-start.6) | collective-permute-done | bytes 131104 | tf_op jit(solution)/shard_map/ppermute | solution.py:438
  53.6 0.6 copy-done.14
  54.2 6.0 %coarse_forward.1 = (bf16[2048,256]{1,0:T(8,128)(2,1)}, f32[2,2048,128]{2,1,0:T(8,128)}, bf16[640,512]{1,0:T(8,128)(2,1)}) custom-call(f32[1,2048,128]{2,1,0:T(8,128)} %get-tuple-element.64.numer0, f32[1,2048,128]{2,1,0:T(8,128)} %get-tuple-element.65.total0, f32[1,2048,128]{2,1,0:T(8,128)} %get-tuple-element.66.numer1, ...), custom_call_target="tpu_custom_call" | custom-call | bytes 300000 | tf_op jit(solution)/shard_map/coarse_forward/pallas_call | solution.py:230
  60.2 4.3 %all-to-all-start = ((bf16[8,256,256]{2,1,0:T(8,128)(2,1)}), bf16[8,256,256]{2,1,0:T(8,128)(2,1)S(1)}, u32[]{:S(2)}, u32[]{:S(2)}) async-start(bf16[8,256,256]{2,1,0:T(8,128)(2,1)} %bitcast.7), calls=%async_computation | async-start | bytes 2097152 | tf_op jit(solution)/shard_map/all_to_all | solution.py:497
  64.9 6.2 %convolution_convert_fusion.1 = bf16[256,2048]{1,0:T(8,128)(2,1)S(1)} fusion(bf16[2048,256]{1,0:T(8,128)(2,1)} %get-tuple-element.76.att_ref, bf16[2048,2048]{1,0:T(8,128)(2,1)} %all-gather.3.cloned.1.call-done), kind=kOutput, calls=%fused_computation.1 | convolution fusion | flops 2148007936 | bytes 10485760 | tf_op jit(solution)/shard_map/dot_general | solution.py:29
  71.2 1.7 %collective-permute-start.7 = (bf16[256,512]{1,0:T(8,128)(2,1)S(1)}, bf16[256,512]{1,0:T(8,128)(2,1)S(1)}, u32[]{:S(2)}, u32[]{:S(2)}) collective-permute-start(bf16[256,512]{1,0:T(8,128)(2,1)S(1)} %get-tuple-element.121), channel_id=1, source_target_pairs={{0,64},{8,72},{16,80},{24,88},{32,96},{40,104},{48,112},{56,120},{... | collective-permute-start | bytes 786440 | tf_op jit(solution)/shard_map/ppermute | solution.py:438
  73.3 1.5 collective-permute-start.9
  74.8 3.4 %fusion.ga_ref = bf16[2048,256]{1,0:T(8,128)(2,1)} fusion(bf16[256,2048]{1,0:T(8,128)(2,1)S(1)} %copy-done.2, bf16[2048,2048]{1,0:T(8,128)(2,1)S(1)} %copy-done), kind=kOutput, calls=%fused_computation.2 | convolution fusion | flops 2148007936 | bytes 10485760 | tf_op jit(solution)/shard_map/dot_general | solution.py:25
  78.2 5.9 %coarse_backward.1 = (bf16[2,2048,256]{2,1,0:T(8,128)(2,1)}, bf16[2,2048,256]{2,1,0:T(8,128)(2,1)}, f32[2,128,128]{2,1,0:T(8,128)}, bf16[128,512]{1,0:T(8,128)(2...) custom-call(bf16[2048,256]{1,0:T(8,128)(2,1)} %fusion.ga_ref, ...), custom_call_target="tpu_custom_call" | custom-call | bytes 300000 | tf_op jit(solution)/shard_map/coarse_backward/pallas_call | solution.py:314
  84.1 1.4 collective-permute-done.8
  85.5 1.6 %collective-permute-done.9 = bf16[256,512]{1,0:T(8,128)(2,1)S(1)} collective-permute-done((bf16[256,512]{1,0:T(8,128)(2,1)S(1)}, bf16[256,512]{1,0:T(8,128)(2,1)S(1)}, u32[]{:S(2)}, u32[]{:S(2)}) %collective-permute-start.9) | collective-permute-done | bytes 262176 | tf_op jit(solution)/shard_map/ppermute | solution.py:438
  87.2 1.4 collective-permute-start.10
  88.6 1.5 collective-permute-start.11
  90.1 0.9 slice.180
  91.0 7.0 %local_backward.2 = (bf16[2048,256]{1,0:T(8,128)(2,1)}, bf16[2048,256]{1,0:T(8,128)(2,1)}, bf16[2048,256]{1,0:T(8,128)(2,1)}) custom-call(bf16[2048,256]{1,0:T(8,128)(2,1)} %q_ref.9, bf16[2048,256]{1,0:T(8,128)(2,1)} %k_ref.9, bf16[2048,256]{1,0:T(8,128)(2,1)} %v_ref.9, bf16[2048,256]{1,0:T(8,128)(2,1)} %get-tuple-element.61.qc_ref.q_ref, ...), custom_call_target="tpu_custom_call" | custom-call | bytes 400000 | tf_op jit(solution)/shard_map/local_backward/pallas_call | solution.py:368
  98.0 3.2 %collective-permute-start.13 = (bf16[256,512]{1,0:T(8,128)(2,1)S(1)}, bf16[256,512]{1,0:T(8,128)(2,1)S(1)}, u32[]{:S(2)}, u32[]{:S(2)}) collective-permute-start(bf16[256,512]{1,0:T(8,128)(2,1)S(1)} %pad_maximum_fusion), channel_id=1, source_target_pairs={{0,56},{8,48},{16,40},{24,32},{32,24},{40,16},{48,8},{56,0},{64,12... | collective-permute-start | bytes 786440 | tf_op jit(solution)/shard_map/ppermute | solution.py:438
  101.3 2.7 %collective-permute-start.12 = (bf16[256,512]{1,0:T(8,128)(2,1)S(1)}, bf16[256,512]{1,0:T(8,128)(2,1)S(1)}, u32[]{:S(2)}, u32[]{:S(2)}) collective-permute-start(bf16[256,512]{1,0:T(8,128)(2,1)S(1)} %add_convert_fusion.2), channel_id=1, source_target_pairs={{0,24},{8,16},{16,8},{24,0},{32,56},{40,48},{48,40},{56,32},{64,88... | collective-permute-start | bytes 786440 | tf_op jit(solution)/shard_map/ppermute | solution.py:438
  104.0 7.1 %local_backward.3 = (bf16[2048,256]{1,0:T(8,128)(2,1)}, bf16[2048,256]{1,0:T(8,128)(2,1)}, bf16[2048,256]{1,0:T(8,128)(2,1)}) custom-call(bf16[2048,256]{1,0:T(8,128)(2,1)} %q_ref.9, bf16[2048,256]{1,0:T(8,128)(2,1)} %k_ref.9, bf16[2048,256]{1,0:T(8,128)(2,1)} %v_ref.9, ...), custom_call_target="tpu_custom_call", output_to_operand_aliasing={{0}: (9, {}), {1}: (10, {}), {2}: (11, {})} | custom-call | bytes 400000 | tf_op jit(solution)/shard_map/local_backward/pallas_call | solution.py:368
  111.1 4.3 %collective-permute-done.12 = bf16[256,512]{1,0:T(8,128)(2,1)S(1)} collective-permute-done((bf16[256,512]{1,0:T(8,128)(2,1)S(1)}, bf16[256,512]{1,0:T(8,128)(2,1)S(1)}, u32[]{:S(2)}, u32[]{:S(2)}) %collective-permute-start.12) | collective-permute-done | bytes 262176 | tf_op jit(solution)/shard_map/ppermute | solution.py:438
  115.8 1.1 collective-permute-start.14
  116.8 2.8 %collective-permute-start.15 = (bf16[128,512]{1,0:T(8,128)(2,1)S(1)}, bf16[128,512]{1,0:T(8,128)(2,1)S(1)}, u32[]{:S(2)}, u32[]{:S(2)}) collective-permute-start(bf16[128,512]{1,0:T(8,128)(2,1)S(1)} %get-tuple-element.154), channel_id=1, source_target_pairs={{0,16},{8,24},{16,0},{24,8},{32,48},{40,56},{48,32},{56,40},{64,80... | collective-permute-start | bytes 393224 | tf_op jit(solution)/shard_map/ppermute | solution.py:438
  119.6 1.4 collective-permute-start.16
  120.9 6.7 %mix.1 = bf16[256,2048]{1,0:T(8,128)(2,1)} custom-call(bf16[8,256,256]{2,1,0:T(8,128)(2,1)} %copy-done.1, bf16[2048,2048]{1,0:T(8,128)(2,1)} %all-gather.5.cloned.1.call-done.w_ref), custom_call_target="tpu_custom_call" | custom-call | bytes 300000 | tf_op jit(solution)/shard_map/mix/pallas_call | solution.py:426
  127.6 1.4 collective-permute-done.15.r2
  129.1 4.3 %collective-permute-done.16.r3 = bf16[128,512]{1,0:T(8,128)(2,1)S(1)} collective-permute-done((bf16[128,512]{1,0:T(8,128)(2,1)S(1)}, bf16[128,512]{1,0:T(8,128)(2,1)S(1)}, u32[]{:S(2)}, u32[]{:S(2)}) %collective-permute-start.16) | collective-permute-done | bytes 131104 | tf_op jit(solution)/shard_map/ppermute | solution.py:438
  133.6 4.0 %collective-permute-start.18 = (bf16[256,512]{1,0:T(8,128)(2,1)S(1)}, bf16[256,512]{1,0:T(8,128)(2,1)S(1)}, u32[]{:S(2)}, u32[]{:S(2)}) collective-permute-start(bf16[256,512]{1,0:T(8,128)(2,1)S(1)} %get-tuple-element.118), channel_id=1, source_target_pairs={{0,64},{8,72},{16,80},{24,88},{32,96},{40,104},{48,112},{56,120},{... | collective-permute-start | bytes 786440 | tf_op jit(solution)/shard_map/ppermute | solution.py:443
  137.6 2.1 %collective-permute-start.20 = (bf16[32,512]{1,0:T(8,128)(2,1)S(1)}, bf16[32,512]{1,0:T(8,128)(2,1)S(1)}, u32[]{:S(2)}, u32[]{:S(2)}) collective-permute-start(bf16[32,512]{1,0:T(8,128)(2,1)S(1)} %slice.225), channel_id=1, source_target_pairs={{0,64},{8,72},{16,80},{24,88},{32,96},{40,104},{48,112},{56,120},{... | collective-permute-start | bytes 98312 | tf_op jit(solution)/shard_map/ppermute | solution.py:438
  139.7 5.1 %collective-permute-done.20.across = bf16[32,512]{1,0:T(8,128)(2,1)S(1)} collective-permute-done((bf16[32,512]{1,0:T(8,128)(2,1)S(1)}, bf16[32,512]{1,0:T(8,128)(2,1)S(1)}, u32[]{:S(2)}, u32[]{:S(2)}) %collective-permute-start.20) | collective-permute-done | bytes 32800 | tf_op jit(solution)/shard_map/ppermute | solution.py:438
  144.8 1.1 collective-permute-start.21
  145.9 1.0 collective-permute-start.22
  147.1 3.2 %finish.1 = (bf16[2048,256]{1,0:T(8,128)(2,1)}, bf16[2048,256]{1,0:T(8,128)(2,1)}) custom-call(bf16[2048,256]{1,0:T(8,128)(2,1)} %get-tuple-element.111.dk_ref, bf16[2048,256]{1,0:T(8,128)(2,1)} %get-tuple-element.112.dv_ref, bf16[64,512]{1,0:T(8,128)(2,1)} %copy-done.4, bf16[32,512]{1,0:T(8,128)(2,1)} %copy-done.19, bf16[192,512]{1,0:T(8,128)(2,1)} %copy-done.5, ...), custom_call_target="tpu_custom_call" | custom-call | bytes 200000 | tf_op jit(solution)/shard_map/finish/pallas_call | solution.py:396
  150.4 0.6 collective-permute-done.22
  151.1 1.0 copy-done.3
  (97 shorter events, 2.9 us)
Async XLA Ops:
  7.2 57.8 %all-gather.3.cloned.1.call-start = ((), (), s32[]{:S(2)}) async-start(), calls=%async_computation.1 | async-start | bytes 9437184 | tf_op jit(solution)/shard_map/all_gather | solution.py:481
  7.9 113.0 %all-gather.5.cloned.1.call-start = ((), (), s32[]{:S(2)}) async-start(), calls=%async_computation.2 | async-start | bytes 9437184 | tf_op jit(solution)/shard_map/all_gather | solution.py:482
  15.1 13.5 %collective-permute-start.1 = (bf16[128,512]{1,0:T(8,128)(2,1)}, bf16[128,512]{1,0:T(8,128)(2,1)S(1)}, u32[]{:S(2)}, u32[]{:S(2)}) collective-permute-start(bf16[128,512]{1,0:T(8,128)(2,1)} %get-tuple-element.69), channel_id=1, source_target_pairs={{0,16},{8,24},{16,0},{24,8},{32,48},{40,56},{48,32},{56,40},{64,80... | collective-permute-start | bytes 393224 | tf_op jit(solution)/shard_map/ppermute | solution.py:438
  18.3 10.2 %collective-permute-start.2 = (bf16[128,512]{1,0:T(8,128)(2,1)}, bf16[128,512]{1,0:T(8,128)(2,1)S(1)}, u32[]{:S(2)}, u32[]{:S(2)}) collective-permute-start(bf16[128,512]{1,0:T(8,128)(2,1)} %get-tuple-element.69), channel_id=1, source_target_pairs={{0,24},{8,16},{16,8},{24,0},{32,56},{40,48},{48,40},{56,32},{64,88... | collective-permute-start | bytes 393224 | tf_op jit(solution)/shard_map/ppermute | solution.py:438
  19.8 10.7 %collective-permute-start = (bf16[192,512]{1,0:T(8,128)(2,1)}, bf16[192,512]{1,0:T(8,128)(2,1)S(1)}, u32[]{:S(2)}, u32[]{:S(2)}) collective-permute-start(bf16[192,512]{1,0:T(8,128)(2,1)} %get-tuple-element.68), channel_id=1, source_target_pairs={{0,8},{8,0},{16,24},{24,16},{32,40},{40,32},{48,56},{56,48},{64,72... | collective-permute-start | bytes 589832 | tf_op jit(solution)/shard_map/ppermute | solution.py:438
  28.5 25.1 %copy-start.9 = (bf16[128,512]{1,0:T(8,128)(2,1)}, bf16[128,512]{1,0:T(8,128)(2,1)S(1)}, u32[]{:S(2)}) copy-start(bf16[128,512]{1,0:T(8,128)(2,1)S(1)} %collective-permute-done.1.refs_1_) | copy-start | bytes 393220
  28.5 25.0 %copy-start.10 = (bf16[128,512]{1,0:T(8,128)(2,1)}, bf16[128,512]{1,0:T(8,128)(2,1)S(1)}, u32[]{:S(2)}) copy-start(bf16[128,512]{1,0:T(8,128)(2,1)S(1)} %collective-permute-done.2.refs_2_) | copy-start | bytes 393220
  30.5 23.1 %copy-start.6 = (bf16[192,512]{1,0:T(8,128)(2,1)}, bf16[192,512]{1,0:T(8,128)(2,1)S(1)}, u32[]{:S(2)}) copy-start(bf16[192,512]{1,0:T(8,128)(2,1)S(1)} %collective-permute-done.refs_0_) | copy-start | bytes 589828
  31.3 17.2 %collective-permute-start.3 = (bf16[160,512]{1,0:T(8,128)(2,1)S(1)}, bf16[160,512]{1,0:T(8,128)(2,1)S(1)}, u32[]{:S(2)}, u32[]{:S(2)}) collective-permute-start(bf16[160,512]{1,0:T(8,128)(2,1)S(1)} %get-tuple-element.140), channel_id=1, source_target_pairs={{0,56},{8,48},{16,40},{24,32},{32,24},{40,16},{48,8},{56,0},{64,12... | collective-permute-start | bytes 491528 | tf_op jit(solution)/shard_map/ppermute | solution.py:438
  36.5 6.2 %collective-permute-start.4 = (bf16[96,512]{1,0:T(8,128)(2,1)S(1)}, bf16[96,512]{1,0:T(8,128)(2,1)S(1)}, u32[]{:S(2)}, u32[]{:S(2)}) collective-permute-start(bf16[96,512]{1,0:T(8,128)(2,1)S(1)} %get-tuple-element.139), channel_id=1, source_target_pairs={{0,64},{8,72},{16,80},{24,88},{32,96},{40,104},{48,112},{56,120},{... | collective-permute-start | bytes 294920 | tf_op jit(solution)/shard_map/ppermute | solution.py:438
  37.8 10.7 %collective-permute-start.5 = (bf16[96,512]{1,0:T(8,128)(2,1)S(1)}, bf16[96,512]{1,0:T(8,128)(2,1)S(1)}, u32[]{:S(2)}, u32[]{:S(2)}) collective-permute-start(bf16[96,512]{1,0:T(8,128)(2,1)S(1)} %get-tuple-element.139), channel_id=1, source_target_pairs={{0,120},{8,112},{16,104},{24,96},{32,88},{40,80},{48,72},{56,64},{... | collective-permute-start | bytes 294920 | tf_op jit(solution)/shard_map/ppermute | solution.py:438
  42.7 10.9 %copy-start.12 = (bf16[96,512]{1,0:T(8,128)(2,1)}, bf16[96,512]{1,0:T(8,128)(2,1)S(1)}, u32[]{:S(2)}) copy-start(bf16[96,512]{1,0:T(8,128)(2,1)S(1)} %collective-permute-done.4.refs_4_) | copy-start | bytes 294916
  48.5 5.1 %copy-start.13 = (bf16[96,512]{1,0:T(8,128)(2,1)}, bf16[96,512]{1,0:T(8,128)(2,1)S(1)}, u32[]{:S(2)}) copy-start(bf16[96,512]{1,0:T(8,128)(2,1)S(1)} %collective-permute-done.5.refs_5_) | copy-start | bytes 294916
  48.5 5.1 %copy-start.11 = (bf16[160,512]{1,0:T(8,128)(2,1)}, bf16[160,512]{1,0:T(8,128)(2,1)S(1)}, u32[]{:S(2)}) copy-start(bf16[160,512]{1,0:T(8,128)(2,1)S(1)} %collective-permute-done.3.refs_3_) | copy-start | bytes 491524
  48.5 5.1 %collective-permute-start.6 = (bf16[128,512]{1,0:T(8,128)(2,1)S(1)}, bf16[128,512]{1,0:T(8,128)(2,1)S(1)}, u32[]{:S(2)}, u32[]{:S(2)}) collective-permute-start(bf16[128,512]{1,0:T(8,128)(2,1)S(1)} %constant_dynamic-update-slice_fusion.16), channel_id=1, source_target_pairs={{0,192},{8,200},{16,208},{24,216},{32,224},{40,232},{48,240},{56,2... | collective-permute-start | bytes 393224 | tf_op jit(solution)/shard_map/ppermute | solution.py:438
  53.6 0.6 copy-start.14
  60.2 28.4 %all-to-all-start = ((bf16[8,256,256]{2,1,0:T(8,128)(2,1)}), bf16[8,256,256]{2,1,0:T(8,128)(2,1)S(1)}, u32[]{:S(2)}, u32[]{:S(2)}) async-start(bf16[8,256,256]{2,1,0:T(8,128)(2,1)} %bitcast.7), calls=%async_computation | async-start | bytes 2097152 | tf_op jit(solution)/shard_map/all_to_all | solution.py:497
  64.5 10.3 %copy-start.2 = (bf16[256,2048]{1,0:T(8,128)(2,1)S(1)}, bf16[256,2048]{1,0:T(8,128)(2,1)}, u32[]{:S(2)}) copy-start(bf16[256,2048]{1,0:T(8,128)(2,1)} %param.8) | copy-start | bytes 3145732
  64.9 9.9 %copy-start = (bf16[2048,2048]{1,0:T(8,128)(2,1)S(1)}, bf16[2048,2048]{1,0:T(8,128)(2,1)}, u32[]{:S(2)}) copy-start(bf16[2048,2048]{1,0:T(8,128)(2,1)} %all-gather.3.cloned.1.call-done) | copy-start | bytes 25165828
  71.2 12.9 %collective-permute-start.7 = (bf16[256,512]{1,0:T(8,128)(2,1)S(1)}, bf16[256,512]{1,0:T(8,128)(2,1)S(1)}, u32[]{:S(2)}, u32[]{:S(2)}) collective-permute-start(bf16[256,512]{1,0:T(8,128)(2,1)S(1)} %get-tuple-element.121), channel_id=1, source_target_pairs={{0,64},{8,72},{16,80},{24,88},{32,96},{40,104},{48,112},{56,120},{... | collective-permute-start | bytes 786440 | tf_op jit(solution)/shard_map/ppermute | solution.py:438
  72.9 12.6 %collective-permute-start.8 = (bf16[256,512]{1,0:T(8,128)(2,1)S(1)}, bf16[256,512]{1,0:T(8,128)(2,1)S(1)}, u32[]{:S(2)}, u32[]{:S(2)}) collective-permute-start(bf16[256,512]{1,0:T(8,128)(2,1)S(1)} %get-tuple-element.120), channel_id=1, source_target_pairs={{0,128},{8,136},{16,144},{24,152},{32,160},{40,168},{48,176},{56,1... | collective-permute-start | bytes 786440 | tf_op jit(solution)/shard_map/ppermute | solution.py:438
  73.3 13.8 %collective-permute-start.9 = (bf16[256,512]{1,0:T(8,128)(2,1)S(1)}, bf16[256,512]{1,0:T(8,128)(2,1)S(1)}, u32[]{:S(2)}, u32[]{:S(2)}) collective-permute-start(bf16[256,512]{1,0:T(8,128)(2,1)S(1)} %get-tuple-element.119), channel_id=1, source_target_pairs={{0,192},{8,200},{16,208},{24,216},{32,224},{40,232},{48,240},{56,2... | collective-permute-start | bytes 786440 | tf_op jit(solution)/shard_map/ppermute | solution.py:438
  84.1 13.9 %copy-start.18 = (bf16[128,512]{1,0:T(8,128)(2,1)S(1)}, bf16[128,512]{1,0:T(8,128)(2,1)}, u32[]{:S(2)}) copy-start(bf16[128,512]{1,0:T(8,128)(2,1)} %get-tuple-element.92) | copy-start | bytes 393220
  84.1 19.9 %copy-start.17 = (bf16[128,512]{1,0:T(8,128)(2,1)S(1)}, bf16[128,512]{1,0:T(8,128)(2,1)}, u32[]{:S(2)}) copy-start(bf16[128,512]{1,0:T(8,128)(2,1)} %get-tuple-element.103) | copy-start | bytes 393220
  84.1 19.9 %copy-start.16 = (bf16[128,512]{1,0:T(8,128)(2,1)S(1)}, bf16[128,512]{1,0:T(8,128)(2,1)}, u32[]{:S(2)}) copy-start(bf16[128,512]{1,0:T(8,128)(2,1)} %get-tuple-element.104) | copy-start | bytes 393220
  87.2 10.8 %collective-permute-start.10 = (bf16[256,512]{1,0:T(8,128)(2,1)S(1)}, bf16[256,512]{1,0:T(8,128)(2,1)S(1)}, u32[]{:S(2)}, u32[]{:S(2)}) collective-permute-start(bf16[256,512]{1,0:T(8,128)(2,1)S(1)} %add_convert_fusion.3), channel_id=1, source_target_pairs={{0,8},{8,0},{16,24},{24,16},{32,40},{40,32},{48,56},{56,48},{64,72... | collective-permute-start | bytes 786440 | tf_op jit(solution)/shard_map/ppermute | solution.py:438
  88.6 22.5 %copy-start.1 = (bf16[8,256,256]{2,1,0:T(8,128)(2,1)}, bf16[8,256,256]{2,1,0:T(8,128)(2,1)S(1)}, u32[]{:S(2)}) copy-start(bf16[8,256,256]{2,1,0:T(8,128)(2,1)S(1)} %all-to-all-done.att_ref) | copy-start | bytes 3145732
  88.6 9.4 %collective-permute-start.11 = (bf16[128,512]{1,0:T(8,128)(2,1)}, bf16[128,512]{1,0:T(8,128)(2,1)S(1)}, u32[]{:S(2)}, u32[]{:S(2)}) collective-permute-start(bf16[128,512]{1,0:T(8,128)(2,1)} %get-tuple-element.86), channel_id=1, source_target_pairs={{0,192},{8,200},{16,208},{24,216},{32,224},{40,232},{48,240},{56,2... | collective-permute-start | bytes 393224 | tf_op jit(solution)/shard_map/ppermute | solution.py:438
  98.0 17.7 %copy-start.15 = (bf16[128,512]{1,0:T(8,128)(2,1)S(1)}, bf16[128,512]{1,0:T(8,128)(2,1)}, u32[]{:S(2)}) copy-start(bf16[128,512]{1,0:T(8,128)(2,1)} %get-tuple-element.93) | copy-start | bytes 393220
  98.0 13.1 %collective-permute-start.13 = (bf16[256,512]{1,0:T(8,128)(2,1)S(1)}, bf16[256,512]{1,0:T(8,128)(2,1)S(1)}, u32[]{:S(2)}, u32[]{:S(2)}) collective-permute-start(bf16[256,512]{1,0:T(8,128)(2,1)S(1)} %pad_maximum_fusion), channel_id=1, source_target_pairs={{0,56},{8,48},{16,40},{24,32},{32,24},{40,16},{48,8},{56,0},{64,12... | collective-permute-start | bytes 786440 | tf_op jit(solution)/shard_map/ppermute | solution.py:438
  101.3 14.1 %collective-permute-start.12 = (bf16[256,512]{1,0:T(8,128)(2,1)S(1)}, bf16[256,512]{1,0:T(8,128)(2,1)S(1)}, u32[]{:S(2)}, u32[]{:S(2)}) collective-permute-start(bf16[256,512]{1,0:T(8,128)(2,1)S(1)} %add_convert_fusion.2), channel_id=1, source_target_pairs={{0,24},{8,16},{16,8},{24,0},{32,56},{40,48},{48,40},{56,32},{64,88... | collective-permute-start | bytes 786440 | tf_op jit(solution)/shard_map/ppermute | solution.py:438
  115.5 17.8 %collective-permute-start.17 = (bf16[256,512]{1,0:T(8,128)(2,1)S(1)}, bf16[256,512]{1,0:T(8,128)(2,1)S(1)}, u32[]{:S(2)}, u32[]{:S(2)}) collective-permute-start(bf16[256,512]{1,0:T(8,128)(2,1)S(1)} %add_convert_fusion.1), channel_id=1, source_target_pairs={{0,56},{8,48},{16,40},{24,32},{32,24},{40,16},{48,8},{56,0},{64,12... | collective-permute-start | bytes 786440 | tf_op jit(solution)/shard_map/ppermute | solution.py:438
  115.8 17.6 %collective-permute-start.14 = (bf16[192,512]{1,0:T(8,128)(2,1)S(1)}, bf16[192,512]{1,0:T(8,128)(2,1)S(1)}, u32[]{:S(2)}, u32[]{:S(2)}) collective-permute-start(bf16[192,512]{1,0:T(8,128)(2,1)S(1)} %get-tuple-element.155), channel_id=1, source_target_pairs={{0,8},{8,0},{16,24},{24,16},{32,40},{40,32},{48,56},{56,48},{64,72... | collective-permute-start | bytes 589832 | tf_op jit(solution)/shard_map/ppermute | solution.py:438
  116.8 12.2 %collective-permute-start.15 = (bf16[128,512]{1,0:T(8,128)(2,1)S(1)}, bf16[128,512]{1,0:T(8,128)(2,1)S(1)}, u32[]{:S(2)}, u32[]{:S(2)}) collective-permute-start(bf16[128,512]{1,0:T(8,128)(2,1)S(1)} %get-tuple-element.154), channel_id=1, source_target_pairs={{0,16},{8,24},{16,0},{24,8},{32,48},{40,56},{48,32},{56,40},{64,80... | collective-permute-start | bytes 393224 | tf_op jit(solution)/shard_map/ppermute | solution.py:438
  119.6 13.7 %collective-permute-start.16 = (bf16[128,512]{1,0:T(8,128)(2,1)S(1)}, bf16[128,512]{1,0:T(8,128)(2,1)S(1)}, u32[]{:S(2)}, u32[]{:S(2)}) collective-permute-start(bf16[128,512]{1,0:T(8,128)(2,1)S(1)} %get-tuple-element.153), channel_id=1, source_target_pairs={{0,24},{8,16},{16,8},{24,0},{32,56},{40,48},{48,40},{56,32},{64,88... | collective-permute-start | bytes 393224 | tf_op jit(solution)/shard_map/ppermute | solution.py:438
  129.1 18.0 %copy-start.7 = (bf16[128,512]{1,0:T(8,128)(2,1)}, bf16[128,512]{1,0:T(8,128)(2,1)S(1)}, u32[]{:S(2)}) copy-start(bf16[128,512]{1,0:T(8,128)(2,1)S(1)} %collective-permute-done.15.r2) | copy-start | bytes 393220
  133.3 13.7 %copy-start.8 = (bf16[128,512]{1,0:T(8,128)(2,1)}, bf16[128,512]{1,0:T(8,128)(2,1)S(1)}, u32[]{:S(2)}) copy-start(bf16[128,512]{1,0:T(8,128)(2,1)S(1)} %collective-permute-done.16.r3) | copy-start | bytes 393220
  133.3 13.7 %copy-start.5 = (bf16[192,512]{1,0:T(8,128)(2,1)}, bf16[192,512]{1,0:T(8,128)(2,1)S(1)}, u32[]{:S(2)}) copy-start(bf16[192,512]{1,0:T(8,128)(2,1)S(1)} %collective-permute-done.14.r1) | copy-start | bytes 589828
  133.6 11.2 %collective-permute-start.18 = (bf16[256,512]{1,0:T(8,128)(2,1)S(1)}, bf16[256,512]{1,0:T(8,128)(2,1)S(1)}, u32[]{:S(2)}, u32[]{:S(2)}) collective-permute-start(bf16[256,512]{1,0:T(8,128)(2,1)S(1)} %get-tuple-element.118), channel_id=1, source_target_pairs={{0,64},{8,72},{16,80},{24,88},{32,96},{40,104},{48,112},{56,120},{... | collective-permute-start | bytes 786440 | tf_op jit(solution)/shard_map/ppermute | solution.py:443
  137.5 7.2 %collective-permute-start.19 = (bf16[256,512]{1,0:T(8,128)(2,1)S(1)}, bf16[256,512]{1,0:T(8,128)(2,1)S(1)}, u32[]{:S(2)}, u32[]{:S(2)}) collective-permute-start(bf16[256,512]{1,0:T(8,128)(2,1)S(1)} %get-tuple-element.118), channel_id=1, source_target_pairs={{0,192},{8,200},{16,208},{24,216},{32,224},{40,232},{48,240},{56,2... | collective-permute-start | bytes 786440 | tf_op jit(solution)/shard_map/ppermute | solution.py:443
  137.6 9.5 %copy-start.4 = (bf16[64,512]{1,0:T(8,128)(2,1)}, bf16[64,512]{1,0:T(8,128)(2,1)S(1)}, u32[]{:S(2)}) copy-start(bf16[64,512]{1,0:T(8,128)(2,1)S(1)} %add_convert_fusion.4.own) | copy-start | bytes 196612
  137.6 7.2 %collective-permute-start.20 = (bf16[32,512]{1,0:T(8,128)(2,1)S(1)}, bf16[32,512]{1,0:T(8,128)(2,1)S(1)}, u32[]{:S(2)}, u32[]{:S(2)}) collective-permute-start(bf16[32,512]{1,0:T(8,128)(2,1)S(1)} %slice.225), channel_id=1, source_target_pairs={{0,64},{8,72},{16,80},{24,88},{32,96},{40,104},{48,112},{56,120},{... | collective-permute-start | bytes 98312 | tf_op jit(solution)/shard_map/ppermute | solution.py:438
  144.8 2.3 %copy-start.19 = (bf16[32,512]{1,0:T(8,128)(2,1)}, bf16[32,512]{1,0:T(8,128)(2,1)S(1)}, u32[]{:S(2)}) copy-start(bf16[32,512]{1,0:T(8,128)(2,1)S(1)} %collective-permute-done.20.across) | copy-start | bytes 98308
  144.8 5.6 %collective-permute-start.21 = (bf16[128,512]{1,0:T(8,128)(2,1)S(1)}, bf16[128,512]{1,0:T(8,128)(2,1)S(1)}, u32[]{:S(2)}, u32[]{:S(2)}) collective-permute-start(bf16[128,512]{1,0:T(8,128)(2,1)S(1)} %slice.211), channel_id=1, source_target_pairs={{0,64},{8,72},{16,80},{24,88},{32,96},{40,104},{48,112},{56,120},{... | collective-permute-start | bytes 393224 | tf_op jit(solution)/shard_map/ppermute | solution.py:443
  145.9 5.0 %collective-permute-start.22 = (bf16[128,512]{1,0:T(8,128)(2,1)S(1)}, bf16[128,512]{1,0:T(8,128)(2,1)S(1)}, u32[]{:S(2)}, u32[]{:S(2)}) collective-permute-start(bf16[128,512]{1,0:T(8,128)(2,1)S(1)} %slice.212), channel_id=1, source_target_pairs={{0,192},{8,200},{16,208},{24,216},{32,224},{40,232},{48,240},{56,2... | collective-permute-start | bytes 393224 | tf_op jit(solution)/shard_map/ppermute | solution.py:443
  151.0 1.0 copy-start.3
Sparse Core Ops, SparseCore 0:
  9.9 55.0 all-gather.2
  66.8 52.4 all-gather.4

commit v2 on v1

--- a/solution.py
+++ b/solution.py
@@ -505,14 +505,14 @@
     mine = after(mine, dq4)
 
     x8 = swap(after(e8, mine), "seq", 24)
-    low = swap(partial, "seq", 1)
+    low = swap(partial, "seq", 3)
     inputs = (queries, keys, values, qc, kc, vc, g0, gc)
     done = local_backward(0, inputs + (after(dq4, partial),))
     low, x8 = after((low, x8), done[0])
     partial = add(partial, low)
 
     f7 = swap(cat([e6, e7[64:], x8[32:64], x8[96:]]), "seq", 7)
-    low = swap(partial, "seq", 3)
+    low = swap(partial, "seq", 1)
     grad_q, dk, dv = local_backward(1, inputs + (after(dq4, partial, x8),), done)
     low, f7 = after((low, f7), grad_q)
     partial = add(partial, low)

time: 160 us -> 162 us (1.012)
  starting transfers between devices: 42.4 us -> 45.1 us
    ppermute x19, starting transfers between devices: 31.9 us -> 34.4 us  [swap(): lax.ppermute(x, axis, [(i, i ^ distance) for i in range(lax.axis_size(axi...]
  transfers between devices with their start and end apart: 26 -> 26, of which waited for: 12 -> 13; matrix products, arithmetic and copies ran while one was open for 8% -> 8% of each run, Pallas kernels for 32% -> 32%
where the time goes in v2:
time: 162 us
  Pallas kernels  51.4 us (32%)
  starting transfers between devices  45.1 us (28%)
  waiting for transfers between devices  35.5 us (22%)
  between operations  14.5 us (9%)
  matrix products  9.55 us (6%)
  local copies, waits for them, and re-layouts  5.1 us (3%)
    ppermute x19, starting transfers between devices, swap(): lax.ppermute(x, axis, [(i, i ^ distance) for i in range(lax.axis_size(axi...  34.4 us
    ppermute x19, waiting for transfers between devices, swap(): lax.ppermute(x, axis, [(i, i ^ distance) for i in range(lax.axis_size(axi...  32.1 us
    pallas_call x2, Pallas kernels, local_backward(): call(local_backward_kernel, 8, grid=(1,), in_specs=[columns] * 6 + [wide]...  14.1 us
    pallas_call x2, Pallas kernels, local_forward(): call(local_forward_kernel, 5, grid=(1,), in_specs=[columns] * 6, out_spec...  9.06 us
    pallas_call x1, Pallas kernels, mix(): call(mix_kernel, 6, in_specs=[whole, pl.BlockSpec(memory_space=pl.ANY)],...  6.66 us
    pallas_call x1, Pallas kernels, coarsen(): call(coarsen_kernel, 6, grid=(width // HD,), in_specs=[spec(tokens)] * 3,...  6.41 us
    ppermute x4, starting transfers between devices, shift_y(): lax.ppermute(x, 'seq', [(i, (i + 8 * distance) % n) for i in range(n)])  6.35 us
    dot_general x1, matrix products, tn(): lax.dot_general(a, b, (((0,), (0,)), ((), ())), preferred_element_type=F32)  6.19 us
  transfers between devices with their start and end apart: 26, of which 13 were waited for; matrix products, arithmetic and copies ran while one was open for 8% of the time, Pallas kernels for 32%

profile of v2, /device:TPU:16, one launch (start us, length us, event | category | flops | bytes accessed | tf_op | source)
XLA Modules:
  0.0 161.7 jit_solution(4637172553323011958)
XLA Ops:
  7.2 0.7 all-gather.3.cloned.1.call-update
  7.9 0.7 all-gather.5.cloned.1.call-update
  8.6 6.4 %coarsen.1 = (bf16[2048,256]{1,0:T(8,128)(2,1)}, bf16[2048,256]{1,0:T(8,128)(2,1)}, bf16[2048,256]{1,0:T(8,128)(2,1)}, bf16[192,512]{1,0:T(8,128)(2,1)}, bf16[128,512]{1,0:T(8,128)(2,1)}) custom-call(bf16[2048,256]{1,0:T(8,128)(2,1)} %q_ref.9, bf16[2048,256]{1,0:T(8,128)(2,1)} %k_ref.9, bf16[2048,256]{1,0:T(8,128)(2,1)} %v_ref.9), custom_call_target="tpu_custom_call" | custom-call | bytes 300000 | tf_op jit(solution)/shard_map/coarsen/pallas_call | solution.py:106
  15.1 3.3 %collective-permute-start.1 = (bf16[128,512]{1,0:T(8,128)(2,1)}, bf16[128,512]{1,0:T(8,128)(2,1)S(1)}, u32[]{:S(2)}, u32[]{:S(2)}) collective-permute-start(bf16[128,512]{1,0:T(8,128)(2,1)} %get-tuple-element.69), channel_id=1, source_target_pairs={{0,16},{8,24},{16,0},{24,8},{32,48},{40,56},{48,32},{56,40},{64,80... | collective-permute-start | bytes 393224 | tf_op jit(solution)/shard_map/ppermute | solution.py:438
  18.3 1.4 collective-permute-start.2
  20.3 4.4 %local_forward.2 = (f32[1,2048,128]{2,1,0:T(8,128)}, f32[1,2048,128]{2,1,0:T(8,128)}) custom-call(bf16[2048,256]{1,0:T(8,128)(2,1)} %q_ref.9, bf16[2048,256]{1,0:T(8,128)(2,1)} %k_ref.9, bf16[2048,256]{1,0:T(8,128)(2,1)} %v_ref.9, bf16[2048,256]{1,0:T(8,128)(2,1)} %get-tuple-element.61.qc_ref.q_ref, bf16[2048,256]{1,0:T(8,128)(2,1)} %get-tuple-element.62.kc_ref, ...), custom_call_target="tpu_custom_call" | custom-call | bytes 250000 | tf_op jit(solution)/shard_map/local_forward/pallas_call | solution.py:160
  24.7 0.8 constant_dynamic-update-slice_fusion.7
  25.5 0.7 constant_dynamic-update-slice_fusion.15
  26.2 2.3 %collective-permute-done.1.refs_1_ = bf16[128,512]{1,0:T(8,128)(2,1)S(1)} collective-permute-done((bf16[128,512]{1,0:T(8,128)(2,1)}, bf16[128,512]{1,0:T(8,128)(2,1)S(1)}, u32[]{:S(2)}, u32[]{:S(2)}) %collective-permute-start.1) | collective-permute-done | bytes 131104 | tf_op jit(solution)/shard_map/ppermute | solution.py:438
  28.5 2.0 %collective-permute-done.refs_0_ = bf16[192,512]{1,0:T(8,128)(2,1)S(1)} collective-permute-done((bf16[192,512]{1,0:T(8,128)(2,1)}, bf16[192,512]{1,0:T(8,128)(2,1)S(1)}, u32[]{:S(2)}, u32[]{:S(2)}) %collective-permute-start) | collective-permute-done | bytes 196640 | tf_op jit(solution)/shard_map/ppermute | solution.py:438
  30.6 0.7 constant_dynamic-update-slice_fusion.22
  31.3 5.2 %collective-permute-start.3 = (bf16[160,512]{1,0:T(8,128)(2,1)S(1)}, bf16[160,512]{1,0:T(8,128)(2,1)S(1)}, u32[]{:S(2)}, u32[]{:S(2)}) collective-permute-start(bf16[160,512]{1,0:T(8,128)(2,1)S(1)} %get-tuple-element.140), channel_id=1, source_target_pairs={{0,56},{8,48},{16,40},{24,32},{32,24},{40,16},{48,8},{56,0},{64,12... | collective-permute-start | bytes 491528 | tf_op jit(solution)/shard_map/ppermute | solution.py:438
  36.5 1.3 collective-permute-start.4
  38.1 4.6 %local_forward.3 = (f32[1,2048,128]{2,1,0:T(8,128)}, f32[1,2048,128]{2,1,0:T(8,128)}) custom-call(bf16[2048,256]{1,0:T(8,128)(2,1)} %q_ref.9, bf16[2048,256]{1,0:T(8,128)(2,1)} %k_ref.9, bf16[2048,256]{1,0:T(8,128)(2,1)} %v_ref.9, bf16[2048,256]{1,0:T(8,128)(2,1)} %get-tuple-element.61.qc_ref.q_ref, bf16[2048,256]{1,0:T(8,128)(2,1)} %get-tuple-element.62.kc_ref, ...), custom_call_target="tpu_custom_call" | custom-call | bytes 250000 | tf_op jit(solution)/shard_map/local_forward/pallas_call | solution.py:160
  42.7 5.8 %collective-permute-done.5.refs_5_ = bf16[96,512]{1,0:T(8,128)(2,1)S(1)} collective-permute-done((bf16[96,512]{1,0:T(8,128)(2,1)S(1)}, bf16[96,512]{1,0:T(8,128)(2,1)S(1)}, u32[]{:S(2)}, u32[]{:S(2)}) %collective-permute-start.5) | collective-permute-done | bytes 98336 | tf_op jit(solution)/shard_map/ppermute | solution.py:438
  48.6 4.9 %collective-permute-done.6.refs_6_ = bf16[128,512]{1,0:T(8,128)(2,1)S(1)} collective-permute-done((bf16[128,512]{1,0:T(8,128)(2,1)S(1)}, bf16[128,512]{1,0:T(8,128)(2,1)S(1)}, u32[]{:S(2)}, u32[]{:S(2)}) %collective-permute-start.6) | collective-permute-done | bytes 131104 | tf_op jit(solution)/shard_map/ppermute | solution.py:438
  53.6 0.6 copy-done.14
  54.2 6.0 %coarse_forward.1 = (bf16[2048,256]{1,0:T(8,128)(2,1)}, f32[2,2048,128]{2,1,0:T(8,128)}, bf16[640,512]{1,0:T(8,128)(2,1)}) custom-call(f32[1,2048,128]{2,1,0:T(8,128)} %get-tuple-element.64.numer0, f32[1,2048,128]{2,1,0:T(8,128)} %get-tuple-element.65.total0, f32[1,2048,128]{2,1,0:T(8,128)} %get-tuple-element.66.numer1, ...), custom_call_target="tpu_custom_call" | custom-call | bytes 300000 | tf_op jit(solution)/shard_map/coarse_forward/pallas_call | solution.py:230
  60.2 4.3 %all-to-all-start = ((bf16[8,256,256]{2,1,0:T(8,128)(2,1)}), bf16[8,256,256]{2,1,0:T(8,128)(2,1)S(1)}, u32[]{:S(2)}, u32[]{:S(2)}) async-start(bf16[8,256,256]{2,1,0:T(8,128)(2,1)} %bitcast.7), calls=%async_computation | async-start | bytes 2097152 | tf_op jit(solution)/shard_map/all_to_all | solution.py:497
  64.9 6.2 %convolution_convert_fusion.1 = bf16[256,2048]{1,0:T(8,128)(2,1)S(1)} fusion(bf16[2048,256]{1,0:T(8,128)(2,1)} %get-tuple-element.76.att_ref, bf16[2048,2048]{1,0:T(8,128)(2,1)} %all-gather.3.cloned.1.call-done), kind=kOutput, calls=%fused_computation.1 | convolution fusion | flops 2148007936 | bytes 10485760 | tf_op jit(solution)/shard_map/dot_general | solution.py:29
  71.2 1.7 %collective-permute-start.7 = (bf16[256,512]{1,0:T(8,128)(2,1)S(1)}, bf16[256,512]{1,0:T(8,128)(2,1)S(1)}, u32[]{:S(2)}, u32[]{:S(2)}) collective-permute-start(bf16[256,512]{1,0:T(8,128)(2,1)S(1)} %get-tuple-element.121), channel_id=1, source_target_pairs={{0,64},{8,72},{16,80},{24,88},{32,96},{40,104},{48,112},{56,120},{... | collective-permute-start | bytes 786440 | tf_op jit(solution)/shard_map/ppermute | solution.py:438
  73.3 1.5 collective-permute-start.9
  74.8 3.4 %fusion.ga_ref = bf16[2048,256]{1,0:T(8,128)(2,1)} fusion(bf16[256,2048]{1,0:T(8,128)(2,1)S(1)} %copy-done.2, bf16[2048,2048]{1,0:T(8,128)(2,1)S(1)} %copy-done), kind=kOutput, calls=%fused_computation.2 | convolution fusion | flops 2148007936 | bytes 10485760 | tf_op jit(solution)/shard_map/dot_general | solution.py:25
  78.2 5.9 %coarse_backward.1 = (bf16[2,2048,256]{2,1,0:T(8,128)(2,1)}, bf16[2,2048,256]{2,1,0:T(8,128)(2,1)}, f32[2,128,128]{2,1,0:T(8,128)}, bf16[128,512]{1,0:T(8,128)(2...) custom-call(bf16[2048,256]{1,0:T(8,128)(2,1)} %fusion.ga_ref, ...), custom_call_target="tpu_custom_call" | custom-call | bytes 300000 | tf_op jit(solution)/shard_map/coarse_backward/pallas_call | solution.py:314
  84.1 1.4 collective-permute-done.8
  85.5 1.6 collective-permute-done.9
  87.2 3.4 %collective-permute-start.10 = (bf16[256,512]{1,0:T(8,128)(2,1)S(1)}, bf16[256,512]{1,0:T(8,128)(2,1)S(1)}, u32[]{:S(2)}, u32[]{:S(2)}) collective-permute-start(bf16[256,512]{1,0:T(8,128)(2,1)S(1)} %add_convert_fusion.3), channel_id=1, source_target_pairs={{0,24},{8,16},{16,8},{24,0},{32,56},{40,48},{48,40},{56,32},{64,88... | collective-permute-start | bytes 786440 | tf_op jit(solution)/shard_map/ppermute | solution.py:438
  90.6 1.5 collective-permute-start.11
  92.1 0.8 slice.180
  92.9 7.1 %local_backward.2 = (bf16[2048,256]{1,0:T(8,128)(2,1)}, bf16[2048,256]{1,0:T(8,128)(2,1)}, bf16[2048,256]{1,0:T(8,128)(2,1)}) custom-call(bf16[2048,256]{1,0:T(8,128)(2,1)} %q_ref.9, bf16[2048,256]{1,0:T(8,128)(2,1)} %k_ref.9, bf16[2048,256]{1,0:T(8,128)(2,1)} %v_ref.9, bf16[2048,256]{1,0:T(8,128)(2,1)} %get-tuple-element.61.qc_ref.q_ref, ...), custom_call_target="tpu_custom_call" | custom-call | bytes 400000 | tf_op jit(solution)/shard_map/local_backward/pallas_call | solution.py:368
  100.1 2.9 %collective-permute-start.13 = (bf16[256,512]{1,0:T(8,128)(2,1)S(1)}, bf16[256,512]{1,0:T(8,128)(2,1)S(1)}, u32[]{:S(2)}, u32[]{:S(2)}) collective-permute-start(bf16[256,512]{1,0:T(8,128)(2,1)S(1)} %pad_maximum_fusion), channel_id=1, source_target_pairs={{0,56},{8,48},{16,40},{24,32},{32,24},{40,16},{48,8},{56,0},{64,12... | collective-permute-start | bytes 786440 | tf_op jit(solution)/shard_map/ppermute | solution.py:438
  103.1 2.8 %collective-permute-start.12 = (bf16[256,512]{1,0:T(8,128)(2,1)S(1)}, bf16[256,512]{1,0:T(8,128)(2,1)S(1)}, u32[]{:S(2)}, u32[]{:S(2)}) collective-permute-start(bf16[256,512]{1,0:T(8,128)(2,1)S(1)} %add_convert_fusion.2), channel_id=1, source_target_pairs={{0,8},{8,0},{16,24},{24,16},{32,40},{40,32},{48,56},{56,48},{64,72... | collective-permute-start | bytes 786440 | tf_op jit(solution)/shard_map/ppermute | solution.py:438
  106.0 7.0 %local_backward.3 = (bf16[2048,256]{1,0:T(8,128)(2,1)}, bf16[2048,256]{1,0:T(8,128)(2,1)}, bf16[2048,256]{1,0:T(8,128)(2,1)}) custom-call(bf16[2048,256]{1,0:T(8,128)(2,1)} %q_ref.9, bf16[2048,256]{1,0:T(8,128)(2,1)} %k_ref.9, bf16[2048,256]{1,0:T(8,128)(2,1)} %v_ref.9, ...), custom_call_target="tpu_custom_call", output_to_operand_aliasing={{0}: (9, {}), {1}: (10, {}), {2}: (11, {})} | custom-call | bytes 400000 | tf_op jit(solution)/shard_map/local_backward/pallas_call | solution.py:368
  113.0 0.6 collective-permute-done.13
  113.6 2.7 %collective-permute-done.12 = bf16[256,512]{1,0:T(8,128)(2,1)S(1)} collective-permute-done((bf16[256,512]{1,0:T(8,128)(2,1)S(1)}, bf16[256,512]{1,0:T(8,128)(2,1)S(1)}, u32[]{:S(2)}, u32[]{:S(2)}) %collective-permute-start.12) | collective-permute-done | bytes 262176 | tf_op jit(solution)/shard_map/ppermute | solution.py:438
  116.6 3.0 %collective-permute-start.14 = (bf16[192,512]{1,0:T(8,128)(2,1)S(1)}, bf16[192,512]{1,0:T(8,128)(2,1)S(1)}, u32[]{:S(2)}, u32[]{:S(2)}) collective-permute-start(bf16[192,512]{1,0:T(8,128)(2,1)S(1)} %get-tuple-element.155), channel_id=1, source_target_pairs={{0,8},{8,0},{16,24},{24,16},{32,40},{40,32},{48,56},{56,48},{64,72... | collective-permute-start | bytes 589832 | tf_op jit(solution)/shard_map/ppermute | solution.py:438
  119.6 0.5 collective-permute-start.15
  120.1 2.0 %collective-permute-start.16 = (bf16[128,512]{1,0:T(8,128)(2,1)S(1)}, bf16[128,512]{1,0:T(8,128)(2,1)S(1)}, u32[]{:S(2)}, u32[]{:S(2)}) collective-permute-start(bf16[128,512]{1,0:T(8,128)(2,1)S(1)} %get-tuple-element.153), channel_id=1, source_target_pairs={{0,24},{8,16},{16,8},{24,0},{32,56},{40,48},{48,40},{56,32},{64,88... | collective-permute-start | bytes 393224 | tf_op jit(solution)/shard_map/ppermute | solution.py:438
  122.0 6.7 %mix.1 = bf16[256,2048]{1,0:T(8,128)(2,1)} custom-call(bf16[8,256,256]{2,1,0:T(8,128)(2,1)} %copy-done.1, bf16[2048,2048]{1,0:T(8,128)(2,1)} %all-gather.5.cloned.1.call-done.w_ref), custom_call_target="tpu_custom_call" | custom-call | bytes 300000 | tf_op jit(solution)/shard_map/mix/pallas_call | solution.py:426
  128.7 3.1 %collective-permute-done.15.r2 = bf16[128,512]{1,0:T(8,128)(2,1)S(1)} collective-permute-done((bf16[128,512]{1,0:T(8,128)(2,1)S(1)}, bf16[128,512]{1,0:T(8,128)(2,1)S(1)}, u32[]{:S(2)}, u32[]{:S(2)}) %collective-permute-start.15) | collective-permute-done | bytes 131104 | tf_op jit(solution)/shard_map/ppermute | solution.py:438
  131.9 3.2 %collective-permute-done.16.r3 = bf16[128,512]{1,0:T(8,128)(2,1)S(1)} collective-permute-done((bf16[128,512]{1,0:T(8,128)(2,1)S(1)}, bf16[128,512]{1,0:T(8,128)(2,1)S(1)}, u32[]{:S(2)}, u32[]{:S(2)}) %collective-permute-start.16) | collective-permute-done | bytes 131104 | tf_op jit(solution)/shard_map/ppermute | solution.py:438
  135.3 2.5 %collective-permute-start.18 = (bf16[256,512]{1,0:T(8,128)(2,1)S(1)}, bf16[256,512]{1,0:T(8,128)(2,1)S(1)}, u32[]{:S(2)}, u32[]{:S(2)}) collective-permute-start(bf16[256,512]{1,0:T(8,128)(2,1)S(1)} %get-tuple-element.118), channel_id=1, source_target_pairs={{0,64},{8,72},{16,80},{24,88},{32,96},{40,104},{48,112},{56,120},{... | collective-permute-start | bytes 786440 | tf_op jit(solution)/shard_map/ppermute | solution.py:443
  137.9 2.5 %collective-permute-start.20 = (bf16[32,512]{1,0:T(8,128)(2,1)S(1)}, bf16[32,512]{1,0:T(8,128)(2,1)S(1)}, u32[]{:S(2)}, u32[]{:S(2)}) collective-permute-start(bf16[32,512]{1,0:T(8,128)(2,1)S(1)} %slice.225), channel_id=1, source_target_pairs={{0,64},{8,72},{16,80},{24,88},{32,96},{40,104},{48,112},{56,120},{... | collective-permute-start | bytes 98312 | tf_op jit(solution)/shard_map/ppermute | solution.py:438
  140.4 4.5 %collective-permute-done.20.across = bf16[32,512]{1,0:T(8,128)(2,1)S(1)} collective-permute-done((bf16[32,512]{1,0:T(8,128)(2,1)S(1)}, bf16[32,512]{1,0:T(8,128)(2,1)S(1)}, u32[]{:S(2)}, u32[]{:S(2)}) %collective-permute-start.20) | collective-permute-done | bytes 32800 | tf_op jit(solution)/shard_map/ppermute | solution.py:438
  145.0 3.8 %collective-permute-start.21 = (bf16[128,512]{1,0:T(8,128)(2,1)S(1)}, bf16[128,512]{1,0:T(8,128)(2,1)S(1)}, u32[]{:S(2)}, u32[]{:S(2)}) collective-permute-start(bf16[128,512]{1,0:T(8,128)(2,1)S(1)} %slice.211), channel_id=1, source_target_pairs={{0,64},{8,72},{16,80},{24,88},{32,96},{40,104},{48,112},{56,120},{... | collective-permute-start | bytes 393224 | tf_op jit(solution)/shard_map/ppermute | solution.py:443
  148.9 3.2 %finish.1 = (bf16[2048,256]{1,0:T(8,128)(2,1)}, bf16[2048,256]{1,0:T(8,128)(2,1)}) custom-call(bf16[2048,256]{1,0:T(8,128)(2,1)} %get-tuple-element.111.dk_ref, bf16[2048,256]{1,0:T(8,128)(2,1)} %get-tuple-element.112.dv_ref, bf16[64,512]{1,0:T(8,128)(2,1)} %copy-done.4, bf16[32,512]{1,0:T(8,128)(2,1)} %copy-done.19, bf16[192,512]{1,0:T(8,128)(2,1)} %copy-done.5, ...), custom_call_target="tpu_custom_call" | custom-call | bytes 200000 | tf_op jit(solution)/shard_map/finish/pallas_call | solution.py:396
  152.2 1.6 collective-permute-done.22
  153.9 1.0 copy-done.3
  (97 shorter events, 3.0 us)
Async XLA Ops:
  7.2 57.8 %all-gather.3.cloned.1.call-start = ((), (), s32[]{:S(2)}) async-start(), calls=%async_computation.1 | async-start | bytes 9437184 | tf_op jit(solution)/shard_map/all_gather | solution.py:481
  7.9 114.1 %all-gather.5.cloned.1.call-start = ((), (), s32[]{:S(2)}) async-start(), calls=%async_computation.2 | async-start | bytes 9437184 | tf_op jit(solution)/shard_map/all_gather | solution.py:482
  15.1 13.5 %collective-permute-start.1 = (bf16[128,512]{1,0:T(8,128)(2,1)}, bf16[128,512]{1,0:T(8,128)(2,1)S(1)}, u32[]{:S(2)}, u32[]{:S(2)}) collective-permute-start(bf16[128,512]{1,0:T(8,128)(2,1)} %get-tuple-element.69), channel_id=1, source_target_pairs={{0,16},{8,24},{16,0},{24,8},{32,48},{40,56},{48,32},{56,40},{64,80... | collective-permute-start | bytes 393224 | tf_op jit(solution)/shard_map/ppermute | solution.py:438
  18.3 10.2 %collective-permute-start.2 = (bf16[128,512]{1,0:T(8,128)(2,1)}, bf16[128,512]{1,0:T(8,128)(2,1)S(1)}, u32[]{:S(2)}, u32[]{:S(2)}) collective-permute-start(bf16[128,512]{1,0:T(8,128)(2,1)} %get-tuple-element.69), channel_id=1, source_target_pairs={{0,24},{8,16},{16,8},{24,0},{32,56},{40,48},{48,40},{56,32},{64,88... | collective-permute-start | bytes 393224 | tf_op jit(solution)/shard_map/ppermute | solution.py:438
  19.8 10.7 %collective-permute-start = (bf16[192,512]{1,0:T(8,128)(2,1)}, bf16[192,512]{1,0:T(8,128)(2,1)S(1)}, u32[]{:S(2)}, u32[]{:S(2)}) collective-permute-start(bf16[192,512]{1,0:T(8,128)(2,1)} %get-tuple-element.68), channel_id=1, source_target_pairs={{0,8},{8,0},{16,24},{24,16},{32,40},{40,32},{48,56},{56,48},{64,72... | collective-permute-start | bytes 589832 | tf_op jit(solution)/shard_map/ppermute | solution.py:438
  28.5 25.1 %copy-start.9 = (bf16[128,512]{1,0:T(8,128)(2,1)}, bf16[128,512]{1,0:T(8,128)(2,1)S(1)}, u32[]{:S(2)}) copy-start(bf16[128,512]{1,0:T(8,128)(2,1)S(1)} %collective-permute-done.1.refs_1_) | copy-start | bytes 393220
  28.5 25.0 %copy-start.10 = (bf16[128,512]{1,0:T(8,128)(2,1)}, bf16[128,512]{1,0:T(8,128)(2,1)S(1)}, u32[]{:S(2)}) copy-start(bf16[128,512]{1,0:T(8,128)(2,1)S(1)} %collective-permute-done.2.refs_2_) | copy-start | bytes 393220
  30.5 23.1 %copy-start.6 = (bf16[192,512]{1,0:T(8,128)(2,1)}, bf16[192,512]{1,0:T(8,128)(2,1)S(1)}, u32[]{:S(2)}) copy-start(bf16[192,512]{1,0:T(8,128)(2,1)S(1)} %collective-permute-done.refs_0_) | copy-start | bytes 589828
  31.3 17.2 %collective-permute-start.3 = (bf16[160,512]{1,0:T(8,128)(2,1)S(1)}, bf16[160,512]{1,0:T(8,128)(2,1)S(1)}, u32[]{:S(2)}, u32[]{:S(2)}) collective-permute-start(bf16[160,512]{1,0:T(8,128)(2,1)S(1)} %get-tuple-element.140), channel_id=1, source_target_pairs={{0,56},{8,48},{16,40},{24,32},{32,24},{40,16},{48,8},{56,0},{64,12... | collective-permute-start | bytes 491528 | tf_op jit(solution)/shard_map/ppermute | solution.py:438
  36.5 6.2 %collective-permute-start.4 = (bf16[96,512]{1,0:T(8,128)(2,1)S(1)}, bf16[96,512]{1,0:T(8,128)(2,1)S(1)}, u32[]{:S(2)}, u32[]{:S(2)}) collective-permute-start(bf16[96,512]{1,0:T(8,128)(2,1)S(1)} %get-tuple-element.139), channel_id=1, source_target_pairs={{0,64},{8,72},{16,80},{24,88},{32,96},{40,104},{48,112},{56,120},{... | collective-permute-start | bytes 294920 | tf_op jit(solution)/shard_map/ppermute | solution.py:438
  37.8 10.7 %collective-permute-start.5 = (bf16[96,512]{1,0:T(8,128)(2,1)S(1)}, bf16[96,512]{1,0:T(8,128)(2,1)S(1)}, u32[]{:S(2)}, u32[]{:S(2)}) collective-permute-start(bf16[96,512]{1,0:T(8,128)(2,1)S(1)} %get-tuple-element.139), channel_id=1, source_target_pairs={{0,120},{8,112},{16,104},{24,96},{32,88},{40,80},{48,72},{56,64},{... | collective-permute-start | bytes 294920 | tf_op jit(solution)/shard_map/ppermute | solution.py:438
  42.7 10.9 %copy-start.12 = (bf16[96,512]{1,0:T(8,128)(2,1)}, bf16[96,512]{1,0:T(8,128)(2,1)S(1)}, u32[]{:S(2)}) copy-start(bf16[96,512]{1,0:T(8,128)(2,1)S(1)} %collective-permute-done.4.refs_4_) | copy-start | bytes 294916
  48.5 5.1 %copy-start.13 = (bf16[96,512]{1,0:T(8,128)(2,1)}, bf16[96,512]{1,0:T(8,128)(2,1)S(1)}, u32[]{:S(2)}) copy-start(bf16[96,512]{1,0:T(8,128)(2,1)S(1)} %collective-permute-done.5.refs_5_) | copy-start | bytes 294916
  48.5 5.1 %copy-start.11 = (bf16[160,512]{1,0:T(8,128)(2,1)}, bf16[160,512]{1,0:T(8,128)(2,1)S(1)}, u32[]{:S(2)}) copy-start(bf16[160,512]{1,0:T(8,128)(2,1)S(1)} %collective-permute-done.3.refs_3_) | copy-start | bytes 491524
  48.5 5.1 %collective-permute-start.6 = (bf16[128,512]{1,0:T(8,128)(2,1)S(1)}, bf16[128,512]{1,0:T(8,128)(2,1)S(1)}, u32[]{:S(2)}, u32[]{:S(2)}) collective-permute-start(bf16[128,512]{1,0:T(8,128)(2,1)S(1)} %constant_dynamic-update-slice_fusion.16), channel_id=1, source_target_pairs={{0,192},{8,200},{16,208},{24,216},{32,224},{40,232},{48,240},{56,2... | collective-permute-start | bytes 393224 | tf_op jit(solution)/shard_map/ppermute | solution.py:438
  53.6 0.6 copy-start.14
  60.2 30.4 %all-to-all-start = ((bf16[8,256,256]{2,1,0:T(8,128)(2,1)}), bf16[8,256,256]{2,1,0:T(8,128)(2,1)S(1)}, u32[]{:S(2)}, u32[]{:S(2)}) async-start(bf16[8,256,256]{2,1,0:T(8,128)(2,1)} %bitcast.7), calls=%async_computation | async-start | bytes 2097152 | tf_op jit(solution)/shard_map/all_to_all | solution.py:497
  64.5 10.3 %copy-start.2 = (bf16[256,2048]{1,0:T(8,128)(2,1)S(1)}, bf16[256,2048]{1,0:T(8,128)(2,1)}, u32[]{:S(2)}) copy-start(bf16[256,2048]{1,0:T(8,128)(2,1)} %param.8) | copy-start | bytes 3145732
  64.9 9.9 %copy-start = (bf16[2048,2048]{1,0:T(8,128)(2,1)S(1)}, bf16[2048,2048]{1,0:T(8,128)(2,1)}, u32[]{:S(2)}) copy-start(bf16[2048,2048]{1,0:T(8,128)(2,1)} %all-gather.3.cloned.1.call-done) | copy-start | bytes 25165828
  71.2 12.9 %collective-permute-start.7 = (bf16[256,512]{1,0:T(8,128)(2,1)S(1)}, bf16[256,512]{1,0:T(8,128)(2,1)S(1)}, u32[]{:S(2)}, u32[]{:S(2)}) collective-permute-start(bf16[256,512]{1,0:T(8,128)(2,1)S(1)} %get-tuple-element.121), channel_id=1, source_target_pairs={{0,64},{8,72},{16,80},{24,88},{32,96},{40,104},{48,112},{56,120},{... | collective-permute-start | bytes 786440 | tf_op jit(solution)/shard_map/ppermute | solution.py:438
  72.9 12.6 %collective-permute-start.8 = (bf16[256,512]{1,0:T(8,128)(2,1)S(1)}, bf16[256,512]{1,0:T(8,128)(2,1)S(1)}, u32[]{:S(2)}, u32[]{:S(2)}) collective-permute-start(bf16[256,512]{1,0:T(8,128)(2,1)S(1)} %get-tuple-element.120), channel_id=1, source_target_pairs={{0,128},{8,136},{16,144},{24,152},{32,160},{40,168},{48,176},{56,1... | collective-permute-start | bytes 786440 | tf_op jit(solution)/shard_map/ppermute | solution.py:438
  73.3 13.8 %collective-permute-start.9 = (bf16[256,512]{1,0:T(8,128)(2,1)S(1)}, bf16[256,512]{1,0:T(8,128)(2,1)S(1)}, u32[]{:S(2)}, u32[]{:S(2)}) collective-permute-start(bf16[256,512]{1,0:T(8,128)(2,1)S(1)} %get-tuple-element.119), channel_id=1, source_target_pairs={{0,192},{8,200},{16,208},{24,216},{32,224},{40,232},{48,240},{56,2... | collective-permute-start | bytes 786440 | tf_op jit(solution)/shard_map/ppermute | solution.py:438
  84.1 16.0 %copy-start.18 = (bf16[128,512]{1,0:T(8,128)(2,1)S(1)}, bf16[128,512]{1,0:T(8,128)(2,1)}, u32[]{:S(2)}) copy-start(bf16[128,512]{1,0:T(8,128)(2,1)} %get-tuple-element.92) | copy-start | bytes 393220
  84.1 21.8 %copy-start.17 = (bf16[128,512]{1,0:T(8,128)(2,1)S(1)}, bf16[128,512]{1,0:T(8,128)(2,1)}, u32[]{:S(2)}) copy-start(bf16[128,512]{1,0:T(8,128)(2,1)} %get-tuple-element.103) | copy-start | bytes 393220
  84.1 21.8 %copy-start.16 = (bf16[128,512]{1,0:T(8,128)(2,1)S(1)}, bf16[128,512]{1,0:T(8,128)(2,1)}, u32[]{:S(2)}) copy-start(bf16[128,512]{1,0:T(8,128)(2,1)} %get-tuple-element.104) | copy-start | bytes 393220
  87.2 12.8 %collective-permute-start.10 = (bf16[256,512]{1,0:T(8,128)(2,1)S(1)}, bf16[256,512]{1,0:T(8,128)(2,1)S(1)}, u32[]{:S(2)}, u32[]{:S(2)}) collective-permute-start(bf16[256,512]{1,0:T(8,128)(2,1)S(1)} %add_convert_fusion.3), channel_id=1, source_target_pairs={{0,24},{8,16},{16,8},{24,0},{32,56},{40,48},{48,40},{56,32},{64,88... | collective-permute-start | bytes 786440 | tf_op jit(solution)/shard_map/ppermute | solution.py:438
  90.6 22.4 %copy-start.1 = (bf16[8,256,256]{2,1,0:T(8,128)(2,1)}, bf16[8,256,256]{2,1,0:T(8,128)(2,1)S(1)}, u32[]{:S(2)}) copy-start(bf16[8,256,256]{2,1,0:T(8,128)(2,1)S(1)} %all-to-all-done.att_ref) | copy-start | bytes 3145732
  90.6 9.4 %collective-permute-start.11 = (bf16[128,512]{1,0:T(8,128)(2,1)}, bf16[128,512]{1,0:T(8,128)(2,1)S(1)}, u32[]{:S(2)}, u32[]{:S(2)}) collective-permute-start(bf16[128,512]{1,0:T(8,128)(2,1)} %get-tuple-element.86), channel_id=1, source_target_pairs={{0,192},{8,200},{16,208},{24,216},{32,224},{40,232},{48,240},{56,2... | collective-permute-start | bytes 393224 | tf_op jit(solution)/shard_map/ppermute | solution.py:438
  100.1 16.4 %copy-start.15 = (bf16[128,512]{1,0:T(8,128)(2,1)S(1)}, bf16[128,512]{1,0:T(8,128)(2,1)}, u32[]{:S(2)}) copy-start(bf16[128,512]{1,0:T(8,128)(2,1)} %get-tuple-element.93) | copy-start | bytes 393220
  100.1 13.5 %collective-permute-start.13 = (bf16[256,512]{1,0:T(8,128)(2,1)S(1)}, bf16[256,512]{1,0:T(8,128)(2,1)S(1)}, u32[]{:S(2)}, u32[]{:S(2)}) collective-permute-start(bf16[256,512]{1,0:T(8,128)(2,1)S(1)} %pad_maximum_fusion), channel_id=1, source_target_pairs={{0,56},{8,48},{16,40},{24,32},{32,24},{40,16},{48,8},{56,0},{64,12... | collective-permute-start | bytes 786440 | tf_op jit(solution)/shard_map/ppermute | solution.py:438
  103.1 13.2 %collective-permute-start.12 = (bf16[256,512]{1,0:T(8,128)(2,1)S(1)}, bf16[256,512]{1,0:T(8,128)(2,1)S(1)}, u32[]{:S(2)}, u32[]{:S(2)}) collective-permute-start(bf16[256,512]{1,0:T(8,128)(2,1)S(1)} %add_convert_fusion.2), channel_id=1, source_target_pairs={{0,8},{8,0},{16,24},{24,16},{32,40},{40,32},{48,56},{56,48},{64,72... | collective-permute-start | bytes 786440 | tf_op jit(solution)/shard_map/ppermute | solution.py:438
  116.3 18.8 %collective-permute-start.17 = (bf16[256,512]{1,0:T(8,128)(2,1)S(1)}, bf16[256,512]{1,0:T(8,128)(2,1)S(1)}, u32[]{:S(2)}, u32[]{:S(2)}) collective-permute-start(bf16[256,512]{1,0:T(8,128)(2,1)S(1)} %add_convert_fusion.1), channel_id=1, source_target_pairs={{0,56},{8,48},{16,40},{24,32},{32,24},{40,16},{48,8},{56,0},{64,12... | collective-permute-start | bytes 786440 | tf_op jit(solution)/shard_map/ppermute | solution.py:438
  116.6 18.5 %collective-permute-start.14 = (bf16[192,512]{1,0:T(8,128)(2,1)S(1)}, bf16[192,512]{1,0:T(8,128)(2,1)S(1)}, u32[]{:S(2)}, u32[]{:S(2)}) collective-permute-start(bf16[192,512]{1,0:T(8,128)(2,1)S(1)} %get-tuple-element.155), channel_id=1, source_target_pairs={{0,8},{8,0},{16,24},{24,16},{32,40},{40,32},{48,56},{56,48},{64,72... | collective-permute-start | bytes 589832 | tf_op jit(solution)/shard_map/ppermute | solution.py:438
  119.6 12.3 %collective-permute-start.15 = (bf16[128,512]{1,0:T(8,128)(2,1)S(1)}, bf16[128,512]{1,0:T(8,128)(2,1)S(1)}, u32[]{:S(2)}, u32[]{:S(2)}) collective-permute-start(bf16[128,512]{1,0:T(8,128)(2,1)S(1)} %get-tuple-element.154), channel_id=1, source_target_pairs={{0,16},{8,24},{16,0},{24,8},{32,48},{40,56},{48,32},{56,40},{64,80... | collective-permute-start | bytes 393224 | tf_op jit(solution)/shard_map/ppermute | solution.py:438
  120.1 15.0 %collective-permute-start.16 = (bf16[128,512]{1,0:T(8,128)(2,1)S(1)}, bf16[128,512]{1,0:T(8,128)(2,1)S(1)}, u32[]{:S(2)}, u32[]{:S(2)}) collective-permute-start(bf16[128,512]{1,0:T(8,128)(2,1)S(1)} %get-tuple-element.153), channel_id=1, source_target_pairs={{0,24},{8,16},{16,8},{24,0},{32,56},{40,48},{48,40},{56,32},{64,88... | collective-permute-start | bytes 393224 | tf_op jit(solution)/shard_map/ppermute | solution.py:438
  131.9 17.0 %copy-start.7 = (bf16[128,512]{1,0:T(8,128)(2,1)}, bf16[128,512]{1,0:T(8,128)(2,1)S(1)}, u32[]{:S(2)}) copy-start(bf16[128,512]{1,0:T(8,128)(2,1)S(1)} %collective-permute-done.15.r2) | copy-start | bytes 393220
  135.1 13.8 %copy-start.8 = (bf16[128,512]{1,0:T(8,128)(2,1)}, bf16[128,512]{1,0:T(8,128)(2,1)S(1)}, u32[]{:S(2)}) copy-start(bf16[128,512]{1,0:T(8,128)(2,1)S(1)} %collective-permute-done.16.r3) | copy-start | bytes 393220
  135.1 13.8 %copy-start.5 = (bf16[192,512]{1,0:T(8,128)(2,1)}, bf16[192,512]{1,0:T(8,128)(2,1)S(1)}, u32[]{:S(2)}) copy-start(bf16[192,512]{1,0:T(8,128)(2,1)S(1)} %collective-permute-done.14.r1) | copy-start | bytes 589828
  135.3 9.6 %collective-permute-start.18 = (bf16[256,512]{1,0:T(8,128)(2,1)S(1)}, bf16[256,512]{1,0:T(8,128)(2,1)S(1)}, u32[]{:S(2)}, u32[]{:S(2)}) collective-permute-start(bf16[256,512]{1,0:T(8,128)(2,1)S(1)} %get-tuple-element.118), channel_id=1, source_target_pairs={{0,64},{8,72},{16,80},{24,88},{32,96},{40,104},{48,112},{56,120},{... | collective-permute-start | bytes 786440 | tf_op jit(solution)/shard_map/ppermute | solution.py:443
  137.8 7.1 %collective-permute-start.19 = (bf16[256,512]{1,0:T(8,128)(2,1)S(1)}, bf16[256,512]{1,0:T(8,128)(2,1)S(1)}, u32[]{:S(2)}, u32[]{:S(2)}) collective-permute-start(bf16[256,512]{1,0:T(8,128)(2,1)S(1)} %get-tuple-element.118), channel_id=1, source_target_pairs={{0,192},{8,200},{16,208},{24,216},{32,224},{40,232},{48,240},{56,2... | collective-permute-start | bytes 786440 | tf_op jit(solution)/shard_map/ppermute | solution.py:443
  137.8 11.1 %copy-start.4 = (bf16[64,512]{1,0:T(8,128)(2,1)}, bf16[64,512]{1,0:T(8,128)(2,1)S(1)}, u32[]{:S(2)}) copy-start(bf16[64,512]{1,0:T(8,128)(2,1)S(1)} %add_convert_fusion.4.own) | copy-start | bytes 196612
  137.9 7.1 %collective-permute-start.20 = (bf16[32,512]{1,0:T(8,128)(2,1)S(1)}, bf16[32,512]{1,0:T(8,128)(2,1)S(1)}, u32[]{:S(2)}, u32[]{:S(2)}) collective-permute-start(bf16[32,512]{1,0:T(8,128)(2,1)S(1)} %slice.225), channel_id=1, source_target_pairs={{0,64},{8,72},{16,80},{24,88},{32,96},{40,104},{48,112},{56,120},{... | collective-permute-start | bytes 98312 | tf_op jit(solution)/shard_map/ppermute | solution.py:438
  144.9 4.0 %copy-start.19 = (bf16[32,512]{1,0:T(8,128)(2,1)}, bf16[32,512]{1,0:T(8,128)(2,1)S(1)}, u32[]{:S(2)}) copy-start(bf16[32,512]{1,0:T(8,128)(2,1)S(1)} %collective-permute-done.20.across) | copy-start | bytes 98308
  145.0 7.2 %collective-permute-start.21 = (bf16[128,512]{1,0:T(8,128)(2,1)S(1)}, bf16[128,512]{1,0:T(8,128)(2,1)S(1)}, u32[]{:S(2)}, u32[]{:S(2)}) collective-permute-start(bf16[128,512]{1,0:T(8,128)(2,1)S(1)} %slice.211), channel_id=1, source_target_pairs={{0,64},{8,72},{16,80},{24,88},{32,96},{40,104},{48,112},{56,120},{... | collective-permute-start | bytes 393224 | tf_op jit(solution)/shard_map/ppermute | solution.py:443
  148.8 5.0 %collective-permute-start.22 = (bf16[128,512]{1,0:T(8,128)(2,1)S(1)}, bf16[128,512]{1,0:T(8,128)(2,1)S(1)}, u32[]{:S(2)}, u32[]{:S(2)}) collective-permute-start(bf16[128,512]{1,0:T(8,128)(2,1)S(1)} %slice.212), channel_id=1, source_target_pairs={{0,192},{8,200},{16,208},{24,216},{32,224},{40,232},{48,240},{56,2... | collective-permute-start | bytes 393224 | tf_op jit(solution)/shard_map/ppermute | solution.py:443
  153.9 1.0 copy-start.3
Sparse Core Ops, SparseCore 0:
  9.9 55.0 all-gather.2
  66.8 52.4 all-gather.4
